TPU v7x, 128 devices: a whole 4x4x4 slice. The times are simulated.
128 devices in a mesh: fsdp: 16 (over x, z), ctx: 2 (over core), tp: 4 (over y).
Axes of the slice: x: 4, y: 4, z: 4, core: 2. Of those that a mesh axis runs over, the one named last changes fastest.
Arguments:
- inputs: bfloat16 [16384, 2048], P(('fsdp', 'ctx', 'tp')), may hold values from -6 to 6
- seq_lengths: int32 [16], P('fsdp'), may hold values from 513 to 1024, as said below
- carried_state: float32 [16, 8, 256, 432], P('fsdp', 'tp'), may hold values from -3 to 3
- attn_gain: float32 [2048], replicated, may hold values from 0.1 to 1.9
- query_weight: bfloat16 [2048, 2048], P(('fsdp', 'ctx'), 'tp'), may hold values from -0.125 to 0.125
- key_weight: bfloat16 [2048, 2048], P(('fsdp', 'ctx'), 'tp'), may hold values from -0.125 to 0.125
- value_weight: bfloat16 [2048, 3456], P(('fsdp', 'ctx'), 'tp'), may hold values from -0.125 to 0.125
- swish_weight: bfloat16 [2048, 3456], P(('fsdp', 'ctx'), 'tp'), may hold values from -0.125 to 0.125
- out_weight: bfloat16 [3456, 2048], P('tp', ('fsdp', 'ctx')), may hold values from -0.21875 to 0.21875
- mlp_gain: float32 [2048], replicated, may hold values from 0.1 to 1.9
- gate_weight: bfloat16 [2048, 3456], P(('fsdp', 'ctx'), 'tp'), may hold values from -0.125 to 0.125
- up_weight: bfloat16 [2048, 3456], P(('fsdp', 'ctx'), 'tp'), may hold values from -0.125 to 0.125
- down_weight: bfloat16 [3456, 2048], P('tp', ('fsdp', 'ctx')), may hold values from -0.15625 to 0.15625
- output_grad: bfloat16 [16384, 2048], P(('fsdp', 'ctx')), may hold values from -6 to 6
Outputs:
- outputs: bfloat16 [16384, 2048], P(('fsdp', 'ctx', 'tp'))
- input_grad: float32 [16384, 2048], P(('fsdp', 'ctx', 'tp'))
- attn_gain_grad: float32 [2048], replicated
- query_weight_gradient: float32 [2048, 2048], P(('fsdp', 'ctx'), 'tp')
- key_grad: float32 [2048, 2048], P(('fsdp', 'ctx'), 'tp')
- value_grad: float32 [2048, 3456], P(('fsdp', 'ctx'), 'tp')
- swish_grad: float32 [2048, 3456], P(('fsdp', 'ctx'), 'tp')
- out_weight_grad: float32 [3456, 2048], P('tp', ('fsdp', 'ctx'))
- mlp_gain_grad: float32 [2048], replicated
- gate_grad: float32 [2048, 3456], P(('fsdp', 'ctx'), 'tp')
- up_grad: float32 [2048, 3456], P(('fsdp', 'ctx'), 'tp')
- down_grad: float32 [3456, 2048], P('tp', ('fsdp', 'ctx'))
Inputs may be any that keep to these rules, and one draw needn't show every extreme that they name: `seq_lengths`: one sequence fills all 1024 positions of its slot and one has exactly 513; positions at or past a sequence's length are padding.
All inputs are finite; a program needn't handle non-finite values.
Results may differ from a plain program's by a relative error of at most 0.02.
Values may be sent and summed in bfloat16 or wider, within the bound.
A program may use at most 192 MiB of HBM per device.

v0:
```python
import jax
import jax.numpy as jnp
from jax import lax
from jax.sharding import PartitionSpec as P

KDIM = 256
VDIM = 432


HIGH = lax.Precision.HIGHEST
EPSILON = 1e-05


def prefix(value, axis, join, neutral):
    count, mine = (lax.axis_size(axis), lax.axis_index(axis))
    pieces = jax.tree.map(lambda part: lax.all_gather(part, axis), value)
    so_far = jax.tree.map(
        lambda part, zero: jnp.full_like(part, 0) + jnp.asarray(zero, part.dtype), value, neutral
    )

    def lap(position, so_far):
        longer = join(so_far, jax.tree.map(lambda part: part[position], pieces))
        return jax.tree.map(lambda new, old: jnp.where(position < mine, new, old), longer, so_far)

    return lax.fori_loop(0, count - 1, lap, so_far)


def prefix_2(array, axis, combine, identity):
    devices, position = (lax.axis_size(axis), lax.axis_index(axis))
    everything = jax.tree.map(
        lambda part, kind: lax.all_gather(part.astype(kind), axis),
        array,
        (jnp.bfloat16, jnp.bfloat16),
    )
    start = jax.tree.map(
        lambda part, zero: jnp.broadcast_to(jnp.asarray(zero, part.dtype), part.shape),
        array,
        identity,
    )

    def lap(k, before):
        at = devices - 1 - k
        reached = at > position
        new = combine(
            before, jax.tree.map(lambda part, own: part[at].astype(own.dtype), everything, array)
        )
        return jax.tree.map(lambda a, b: jnp.where(reached, a, b), new, before)

    return lax.fori_loop(0, devices, lap, start)


def layer_norm(rows_in, gain):
    centre = jnp.mean(rows_in, axis=-1, keepdims=True)
    centred = rows_in - centre
    spread = jnp.mean(centred * centred, axis=-1, keepdims=True)
    return centred * lax.rsqrt(spread + EPSILON) * gain


def group_norm(values_in, head_count):
    shaped = values_in.reshape(values_in.shape[0], head_count, -1)
    centre = jnp.mean(shaped, axis=-1, keepdims=True)
    centred = shaped - centre
    spread = jnp.mean(centred * centred, axis=-1, keepdims=True)
    return (centred * lax.rsqrt(spread + EPSILON)).reshape(values_in.shape)


def rotate(field, angles, head_count):
    row_count = field.shape[0]
    half_width = angles.shape[1]
    shaped = field.reshape(row_count, head_count, 2, half_width)
    cosine = jnp.cos(angles)[:, None, :]
    sine = jnp.sin(angles)[:, None, :]
    former = shaped[:, :, 0]
    latter = shaped[:, :, 1]
    turned = jnp.stack([former * cosine - latter * sine, former * sine + latter * cosine], axis=2)
    return turned.reshape(field.shape)


def decay_mask(first_row, row_count, key_count, decays):
    query_pos = (first_row + jnp.arange(row_count)).astype(jnp.float32)
    key_pos = jnp.arange(key_count).astype(jnp.float32)
    distance = query_pos[:, None] - key_pos[None, :]
    factor = jnp.exp(jnp.maximum(distance, 0.0)[None] * decays[:, None, None])
    return jnp.where(distance[None] >= 0.0, factor, 0.0)


def head_decays(head_ids, seq_len):
    return -jnp.power(2.0, 5.0 - head_ids.astype(jnp.float32)) / seq_len


def chain(earlier, later):
    return (earlier[0] * later[1] + later[0], earlier[1] * later[1])


def on_device(
    inputs,
    seq_lengths,
    carried_state,
    attn_gain,
    query_weight,
    key_weight,
    value_weight,
    swish_weight,
    out_weight,
    mlp_gain,
    gate_weight,
    up_weight,
    down_weight,
    output_grad,
):
    heads_dev = query_weight.shape[1] // KDIM
    rows_dev = inputs.shape[0]
    rows_ctx = rows_dev * lax.axis_size("tp")
    seq_len = rows_ctx * lax.axis_size("ctx")
    block_rows = min(512, rows_ctx)
    num_blocks = rows_ctx // block_rows
    position = lax.axis_index("ctx") * rows_ctx + jnp.arange(rows_ctx, dtype=jnp.int32)
    row_mask = (position < seq_lengths[0]).astype(jnp.float32)[:, None]
    half_width = KDIM // 2
    frequency = jnp.power(10000.0, -jnp.arange(half_width).astype(jnp.float32) / half_width)
    angles = position.astype(jnp.float32)[:, None] * frequency[None, :]
    head_ids = lax.axis_index("tp") * heads_dev + jnp.arange(heads_dev, dtype=jnp.int32)
    decays = head_decays(head_ids, seq_len)
    local_pos = jnp.arange(rows_ctx).astype(jnp.float32)
    tail_fac = jnp.exp((rows_ctx - 1.0 - local_pos)[None, :] * decays[:, None])
    head_fac = jnp.exp((local_pos + 1.0)[None, :] * decays[:, None])
    span = jnp.exp(rows_ctx * decays)[:, None, None]
    start_fac = jnp.exp((lax.axis_index("ctx") * rows_ctx).astype(jnp.float32) * decays)[
        :, None, None
    ]
    w_query, w_key, w_value, w_swish, w_out, w_gate, w_up, w_down = (
        lax.all_gather(query_weight, ("fsdp", "ctx"), axis=0, tiled=True),
        lax.all_gather(key_weight, ("fsdp", "ctx"), axis=0, tiled=True),
        lax.all_gather(value_weight, ("fsdp", "ctx"), axis=0, tiled=True),
        lax.all_gather(swish_weight, ("fsdp", "ctx"), axis=0, tiled=True),
        lax.all_gather(out_weight, ("fsdp", "ctx"), axis=1, tiled=True),
        lax.all_gather(gate_weight, ("fsdp", "ctx"), axis=0, tiled=True),
        lax.all_gather(up_weight, ("fsdp", "ctx"), axis=0, tiled=True),
        lax.all_gather(down_weight, ("fsdp", "ctx"), axis=1, tiled=True),
    )
    inputs_wide = inputs.astype(jnp.float32)
    normed_one = layer_norm(inputs_wide, attn_gain).astype(jnp.bfloat16)
    rows_one = lax.all_gather(normed_one, "tp", axis=0, tiled=True)
    query_raw = jnp.dot(rows_one, w_query, preferred_element_type=jnp.float32)
    key_raw = jnp.dot(rows_one, w_key, preferred_element_type=jnp.float32)
    value_raw = jnp.dot(rows_one, w_value, preferred_element_type=jnp.float32)
    swish_raw = jnp.dot(rows_one, w_swish, preferred_element_type=jnp.float32)
    queries = rotate(query_raw, angles, heads_dev).astype(jnp.bfloat16)
    keys_rot = rotate(key_raw, angles, heads_dev).astype(jnp.bfloat16)
    values_kept = (value_raw * row_mask).astype(jnp.bfloat16)
    query_head_split = queries.reshape(rows_ctx, heads_dev, KDIM).transpose(1, 0, 2)
    key_head_split = keys_rot.reshape(rows_ctx, heads_dev, KDIM).transpose(1, 0, 2)
    value_head_split = values_kept.reshape(rows_ctx, heads_dev, VDIM).transpose(1, 0, 2)

    def inner_block(block):
        first_row = block * block_rows
        scores = jnp.einsum(
            "hrk,hsk->hrs", query_head_split, key_head_split, preferred_element_type=jnp.float32
        )
        mixing = (scores * decay_mask(first_row, block_rows, rows_ctx, decays)).astype(jnp.bfloat16)
        return jnp.einsum(
            "hrs,hsv->hrv", mixing, value_head_split, preferred_element_type=jnp.float32
        )

    inner = lax.map(inner_block, jnp.arange(num_blocks))
    inner = inner.transpose(1, 0, 2, 3).reshape(heads_dev, rows_ctx, VDIM)
    local_state = jnp.einsum(
        "tsj,tse->tje",
        key_head_split.astype(jnp.float32) * tail_fac[:, :, None],
        value_head_split.astype(jnp.float32),
        precision=HIGH,
    )
    prior_state, prior_span = prefix(
        (local_state, span), "ctx", chain, (jnp.zeros_like(local_state), jnp.ones_like(span))
    )
    prior_state = start_fac * carried_state[0] + prior_state
    preceding_lowered = prior_state.astype(jnp.bfloat16)
    cross = (
        jnp.einsum(
            "qga,qax->qgx", query_head_split, preceding_lowered, preferred_element_type=jnp.float32
        )
        * head_fac[:, :, None]
    )
    retained = (inner + cross).transpose(1, 0, 2).reshape(rows_ctx, heads_dev * VDIM)

    def gate_piece(swish_in, retained_in):
        return row_mask * jax.nn.silu(swish_in) * group_norm(retained_in, heads_dev)

    mixed = gate_piece(swish_raw, retained).astype(jnp.bfloat16)
    attn_out = lax.psum_scatter(
        jnp.dot(mixed, w_out, preferred_element_type=jnp.float32),
        "tp",
        scatter_dimension=0,
        tiled=True,
    )
    hidden_state = inputs_wide + attn_out
    normed_two = layer_norm(hidden_state, mlp_gain).astype(jnp.bfloat16)
    rows_two = lax.all_gather(normed_two, "tp", axis=0, tiled=True)
    gate_pre = jnp.dot(rows_two, w_gate, preferred_element_type=jnp.float32)
    up_pre = jnp.dot(rows_two, w_up, preferred_element_type=jnp.float32)

    def mlp_piece(gate_in, up_in):
        return jax.nn.gelu(gate_in, approximate=False) * up_in

    activated = mlp_piece(gate_pre, up_pre).astype(jnp.bfloat16)
    mlp_out = lax.psum_scatter(
        jnp.dot(activated, w_down, preferred_element_type=jnp.float32).astype(jnp.bfloat16),
        "tp",
        scatter_dimension=0,
        tiled=True,
    ).astype(jnp.float32)
    outputs = (hidden_state + mlp_out).astype(jnp.bfloat16)
    own_first = lax.axis_index("tp") * rows_dev
    grad_own = lax.dynamic_slice_in_dim(output_grad, own_first, rows_dev, 0).astype(jnp.float32)
    down_part = jnp.dot(activated.T, output_grad, preferred_element_type=jnp.float32)
    grad_act = jnp.dot(output_grad, w_down.T, preferred_element_type=jnp.float32)
    _, mlp_pull = jax.vjp(mlp_piece, gate_pre, up_pre)
    grad_gate, grad_up = mlp_pull(grad_act)
    grad_gate = grad_gate.astype(jnp.bfloat16)
    grad_up = grad_up.astype(jnp.bfloat16)
    gate_part = jnp.dot(rows_two.T, grad_gate, preferred_element_type=jnp.float32)
    up_part = jnp.dot(rows_two.T, grad_up, preferred_element_type=jnp.float32)
    grad_norm_two = lax.psum_scatter(
        jnp.dot(grad_gate, w_gate.T, preferred_element_type=jnp.float32)
        + jnp.dot(grad_up, w_up.T, preferred_element_type=jnp.float32),
        "tp",
        scatter_dimension=0,
        tiled=True,
    )
    _, norm_two_pull = jax.vjp(layer_norm, hidden_state, mlp_gain)
    grad_hidden_norm, mlp_gain_part = norm_two_pull(grad_norm_two)
    grad_hidden = grad_own + grad_hidden_norm
    mid_rows = lax.all_gather(grad_hidden.astype(jnp.bfloat16), "tp", axis=0, tiled=True)
    out_part = jnp.dot(mixed.T, mid_rows, preferred_element_type=jnp.float32)
    grad_mixed = jnp.dot(mid_rows, w_out.T, preferred_element_type=jnp.float32)
    _, gate_pull = jax.vjp(gate_piece, swish_raw, retained)
    grad_swish, grad_retained = gate_pull(grad_mixed)
    grad_swish = grad_swish.astype(jnp.bfloat16)
    head_gradient_rows = (
        grad_retained.astype(jnp.bfloat16).reshape(rows_ctx, heads_dev, VDIM).transpose(1, 0, 2)
    )
    grad_prior = jnp.einsum(
        "tsj,tse->tje",
        query_head_split.astype(jnp.float32) * head_fac[:, :, None],
        head_gradient_rows.astype(jnp.float32),
        precision=HIGH,
    )
    grad_query_cross = (
        jnp.einsum(
            "icu,izu->icz",
            head_gradient_rows,
            preceding_lowered,
            preferred_element_type=jnp.float32,
        )
        * head_fac[:, :, None]
    )
    later_grad, later_span = prefix_2(
        (grad_prior, span), "ctx", chain, (jnp.zeros_like(grad_prior), jnp.ones_like(span))
    )
    following_lowered = later_grad.astype(jnp.bfloat16)
    grad_key_cross = (
        jnp.einsum(
            "icu,izu->icz", value_head_split, following_lowered, preferred_element_type=jnp.float32
        )
        * tail_fac[:, :, None]
    )
    grad_value_cross = (
        jnp.einsum(
            "qga,qax->qgx", key_head_split, following_lowered, preferred_element_type=jnp.float32
        )
        * tail_fac[:, :, None]
    )

    def inner_back(carry, block):
        key_total, value_total = carry
        first_row = block * block_rows
        decay_block = decay_mask(first_row, block_rows, rows_ctx, decays)
        scores = jnp.einsum(
            "hrk,hsk->hrs", query_head_split, key_head_split, preferred_element_type=jnp.float32
        )
        mixing = (scores * decay_block).astype(jnp.bfloat16)
        value_total = value_total + jnp.einsum(
            "hrs,hrv->hsv", mixing, head_gradient_rows, preferred_element_type=jnp.float32
        )
        grad_mixing = jnp.einsum(
            "hrv,hsv->hrs", head_gradient_rows, value_head_split, preferred_element_type=jnp.float32
        )
        grad_scores = (grad_mixing * decay_block).astype(jnp.bfloat16)
        key_total = key_total + jnp.einsum(
            "hrs,hrk->hsk", grad_scores, query_head_split, preferred_element_type=jnp.float32
        )
        query_block_grad = jnp.einsum(
            "hrs,hsk->hrk", grad_scores, key_head_split, preferred_element_type=jnp.float32
        )
        return ((key_total, value_total), query_block_grad)

    (grad_key_heads, grad_value_heads), query_blocks = lax.scan(
        inner_back, (grad_key_cross, grad_value_cross), jnp.arange(num_blocks)
    )
    grad_query_heads = grad_query_cross + query_blocks.transpose(1, 0, 2, 3).reshape(
        heads_dev, rows_ctx, KDIM
    )
    grad_query_raw = rotate(
        grad_query_heads.transpose(1, 0, 2).reshape(rows_ctx, heads_dev * KDIM), -angles, heads_dev
    ).astype(jnp.bfloat16)
    grad_key_raw = rotate(
        grad_key_heads.transpose(1, 0, 2).reshape(rows_ctx, heads_dev * KDIM), -angles, heads_dev
    ).astype(jnp.bfloat16)
    grad_value_raw = (
        grad_value_heads.transpose(1, 0, 2).reshape(rows_ctx, heads_dev * VDIM) * row_mask
    ).astype(jnp.bfloat16)
    query_part = jnp.dot(rows_one.T, grad_query_raw, preferred_element_type=jnp.float32)
    key_part = jnp.dot(rows_one.T, grad_key_raw, preferred_element_type=jnp.float32)
    value_part = jnp.dot(rows_one.T, grad_value_raw, preferred_element_type=jnp.float32)
    swish_part = jnp.dot(rows_one.T, grad_swish, preferred_element_type=jnp.float32)
    total_rows = jnp.dot(grad_query_raw, w_query.T, preferred_element_type=jnp.float32)
    total_rows = total_rows + jnp.dot(grad_key_raw, w_key.T, preferred_element_type=jnp.float32)
    total_rows = total_rows + jnp.dot(grad_value_raw, w_value.T, preferred_element_type=jnp.float32)
    grad_norm_one = lax.psum_scatter(
        (total_rows + jnp.dot(grad_swish, w_swish.T, preferred_element_type=jnp.float32)).astype(
            jnp.bfloat16
        ),
        "tp",
        scatter_dimension=0,
        tiled=True,
    ).astype(jnp.float32)
    _, norm_one_pull = jax.vjp(layer_norm, inputs_wide, attn_gain)
    grad_inputs_norm, attn_gain_part = norm_one_pull(grad_norm_one)
    input_grad = grad_hidden + grad_inputs_norm
    attn_gain_grad, mlp_gain_grad = lax.psum((attn_gain_part, mlp_gain_part), ("fsdp", "ctx", "tp"))
    summed = (
        lax.psum_scatter(
            query_part.astype(jnp.bfloat16), ("fsdp", "ctx"), scatter_dimension=0, tiled=True
        ).astype(jnp.float32),
        lax.psum_scatter(
            key_part.astype(jnp.bfloat16), ("fsdp", "ctx"), scatter_dimension=0, tiled=True
        ).astype(jnp.float32),
        lax.psum_scatter(
            value_part.astype(jnp.bfloat16), ("fsdp", "ctx"), scatter_dimension=0, tiled=True
        ).astype(jnp.float32),
        lax.psum_scatter(
            swish_part.astype(jnp.bfloat16), ("fsdp", "ctx"), scatter_dimension=0, tiled=True
        ).astype(jnp.float32),
        lax.psum_scatter(
            out_part.astype(jnp.bfloat16), ("fsdp", "ctx"), scatter_dimension=1, tiled=True
        ).astype(jnp.float32),
        lax.psum_scatter(
            gate_part.astype(jnp.bfloat16), ("fsdp", "ctx"), scatter_dimension=0, tiled=True
        ).astype(jnp.float32),
        lax.psum_scatter(
            up_part.astype(jnp.bfloat16), ("fsdp", "ctx"), scatter_dimension=0, tiled=True
        ).astype(jnp.float32),
        lax.psum_scatter(
            down_part.astype(jnp.bfloat16), ("fsdp", "ctx"), scatter_dimension=1, tiled=True
        ).astype(jnp.float32),
    )
    return (
        outputs,
        input_grad,
        attn_gain_grad,
        summed[0],
        summed[1],
        summed[2],
        summed[3],
        summed[4],
        mlp_gain_grad,
        summed[5],
        summed[6],
        summed[7],
    )


def solution(mesh):
    placed = (
        P(("fsdp", "ctx", "tp"), None),
        P("fsdp"),
        P("fsdp", "tp", None, None),
        P(),
        P(("fsdp", "ctx"), "tp"),
        P(("fsdp", "ctx"), "tp"),
        P(("fsdp", "ctx"), "tp"),
        P(("fsdp", "ctx"), "tp"),
        P("tp", ("fsdp", "ctx")),
        P(),
        P(("fsdp", "ctx"), "tp"),
        P(("fsdp", "ctx"), "tp"),
        P("tp", ("fsdp", "ctx")),
        P(("fsdp", "ctx"), None),
    )
    return jax.shard_map(
        on_device,
        mesh=mesh,
        in_specs=placed,
        out_specs=(
            P(("fsdp", "ctx", "tp"), None),
            P(("fsdp", "ctx", "tp"), None),
            P(),
            P(("fsdp", "ctx"), "tp"),
            P(("fsdp", "ctx"), "tp"),
            P(("fsdp", "ctx"), "tp"),
            P(("fsdp", "ctx"), "tp"),
            P("tp", ("fsdp", "ctx")),
            P(),
            P(("fsdp", "ctx"), "tp"),
            P(("fsdp", "ctx"), "tp"),
            P("tp", ("fsdp", "ctx")),
        ),
        check_vma=False,
    )
```

profile of v0, /device:TPU:1, one launch (start us, length us, event | category | flops | bytes accessed | tf_op | source)
XLA Modules:
  0.0 1369.5 jit_solution(7886877925193312522)
XLA Ops:
  17.6 28.6 %all-gather.15.cloned.1.call-done = bf16[512,2048]{1,0:T(8,128)(2,1)} async-done(((bf16[128,2048]{1,0:T(8,128)(2,1)}), bf16[512,2048]{1,0:T(8,128)(2,1)}) %all-gather.15.cloned.1.call-update) | async-done | bytes 2097168 | tf_op jit(solution)/shard_map/all_gather | solution.py:143
  46.2 46.7 %all-gather.19.cloned.1.call-done = bf16[2048,512]{1,0:T(8,128)(2,1)} async-done(((bf16[64,512]{1,0:T(8,128)(2,1)}), bf16[2048,512]{1,0:T(8,128)(2,1)}) %all-gather.19.cloned.1.call-update) | async-done | bytes 2097168 | tf_op jit(solution)/shard_map/all_gather | solution.py:132
  96.4 42.0 %all-gather.21.cloned.1.call-done = bf16[2048,512]{1,0:T(8,128)(2,1)} async-done(((bf16[64,512]{1,0:T(8,128)(2,1)}), bf16[2048,512]{1,0:T(8,128)(2,1)}) %all-gather.21.cloned.1.call-update) | async-done | bytes 2097168 | tf_op jit(solution)/shard_map/all_gather | solution.py:133
  142.6 43.1 %all-gather.23.cloned.1.call-done = bf16[2048,864]{1,0:T(8,128)(2,1)} async-done(((bf16[64,864]{1,0:T(8,128)(2,1)}), bf16[2048,864]{1,0:T(8,128)(2,1)}) %all-gather.23.cloned.1.call-update) | async-done | bytes 3538960 | tf_op jit(solution)/shard_map/all_gather | solution.py:134
  210.2 43.9 %all-gather.17.cloned.1.call-done = bf16[2048,864]{1,0:T(8,128)(2,1)} async-done(((bf16[64,864]{1,0:T(8,128)(2,1)}), bf16[2048,864]{1,0:T(8,128)(2,1)}) %all-gather.17.cloned.1.call-update) | async-done | bytes 3538960 | tf_op jit(solution)/shard_map/all_gather | solution.py:135
  260.8 40.8 %all-gather.25.cloned.1.call-done = bf16[864,2048]{0,1:T(8,128)(2,1)} async-done(((bf16[864,64]{0,1:T(8,128)(2,1)}), bf16[864,2048]{0,1:T(8,128)(2,1)}) %all-gather.25.cloned.1.call-update) | async-done | bytes 3538960 | tf_op jit(solution)/shard_map/all_gather | solution.py:136
  308.8 45.1 %reduce-scatter.13.cloned.1.call-done = f32[128,2048]{1,0:T(8,128)} async-done(((f32[512,2048]{1,0:T(8,128)}), f32[128,2048]{1,0:T(8,128)}) %reduce-scatter.13.cloned.1.call-update) | async-done | bytes 1048592 | tf_op jit(solution)/shard_map/reduce_scatter | solution.py:190
  358.4 44.0 %all-gather.29.cloned.1.call-done = bf16[2048,864]{1,0:T(8,128)(2,1)} async-done(((bf16[64,864]{1,0:T(8,128)(2,1)}), bf16[2048,864]{1,0:T(8,128)(2,1)}) %all-gather.29.cloned.1.call-update) | async-done | bytes 3538960 | tf_op jit(solution)/shard_map/all_gather | solution.py:137
  402.5 31.9 %all-gather.27.cloned.1.call-done = bf16[512,2048]{1,0:T(8,128)(2,1)} async-done(((bf16[128,2048]{1,0:T(8,128)(2,1)}), bf16[512,2048]{1,0:T(8,128)(2,1)}) %all-gather.27.cloned.1.call-update) | async-done | bytes 2097168 | tf_op jit(solution)/shard_map/all_gather | solution.py:198
  440.3 42.9 %all-gather.33.cloned.1.call-done = bf16[864,2048]{0,1:T(8,128)(2,1)} async-done(((bf16[864,64]{0,1:T(8,128)(2,1)}), bf16[864,2048]{0,1:T(8,128)(2,1)}) %all-gather.33.cloned.1.call-update) | async-done | bytes 3538960 | tf_op jit(solution)/shard_map/all_gather | solution.py:139
  483.3 10.7 multiply_convert_fusion.2
  494.0 36.8 %all-gather.31.cloned.1.call-done = bf16[2048,864]{1,0:T(8,128)(2,1)} async-done(((bf16[64,864]{1,0:T(8,128)(2,1)}), bf16[2048,864]{1,0:T(8,128)(2,1)}) %all-gather.31.cloned.1.call-update) | async-done | bytes 3538960 | tf_op jit(solution)/shard_map/all_gather | solution.py:138
  552.1 39.7 %reduce-scatter.17.cloned.1.call-done = f32[128,2048]{1,0:T(8,128)} async-done(((f32[512,2048]{1,0:T(8,128)}), f32[128,2048]{1,0:T(8,128)}) %reduce-scatter.17.cloned.1.call-update) | async-done | bytes 1048592 | tf_op jit(solution)/shard_map/reduce_scatter | solution.py:223
  593.5 30.1 %reduce-scatter.15.cloned.1.call-done = bf16[128,2048]{1,0:T(8,128)(2,1)} async-done(((bf16[512,2048]{1,0:T(8,128)(2,1)}), bf16[128,2048]{1,0:T(8,128)(2,1)}) %reduce-scatter.15.cloned.1.call-update) | async-done | bytes 524304 | tf_op jit(solution)/shard_map/reduce_scatter | solution.py:206
  730.7 12.8 reduce-scatter.31.cloned.1.call-done
  745.1 82.5 %reduce-scatter.33.cloned.1.call-done = bf16[64,864]{1,0:T(8,128)(2,1)} async-done(((bf16[2048,864]{1,0:T(8,128)(2,1)}), bf16[64,864]{1,0:T(8,128)(2,1)}) %reduce-scatter.33.cloned.1.call-update) | async-done | bytes 110608 | tf_op jit(solution)/shard_map/reduce_scatter | solution.py:350
  829.2 82.9 %reduce-scatter.35.cloned.1.call-done = bf16[864,64]{0,1:T(8,128)(2,1)} async-done(((bf16[864,2048]{0,1:T(8,128)(2,1)}), bf16[864,64]{0,1:T(8,128)(2,1)}) %reduce-scatter.35.cloned.1.call-update) | async-done | bytes 110608 | tf_op jit(solution)/shard_map/reduce_scatter | solution.py:353
  913.7 80.2 %reduce-scatter.23.cloned.1.call-done = bf16[64,512]{1,0:T(8,128)(2,1)} async-done(((bf16[2048,512]{1,0:T(8,128)(2,1)}), bf16[64,512]{1,0:T(8,128)(2,1)}) %reduce-scatter.23.cloned.1.call-update) | async-done | bytes 65552 | tf_op jit(solution)/shard_map/reduce_scatter | solution.py:335
  995.4 80.1 %reduce-scatter.21.cloned.1.call-done = bf16[64,512]{1,0:T(8,128)(2,1)} async-done(((bf16[2048,512]{1,0:T(8,128)(2,1)}), bf16[64,512]{1,0:T(8,128)(2,1)}) %reduce-scatter.21.cloned.1.call-update) | async-done | bytes 65552 | tf_op jit(solution)/shard_map/reduce_scatter | solution.py:332
  1077.1 31.5 %reduce-scatter.19.cloned.1.call-done = bf16[128,2048]{1,0:T(8,128)(2,1)} async-done(((bf16[512,2048]{1,0:T(8,128)(2,1)}), bf16[128,2048]{1,0:T(8,128)(2,1)}) %reduce-scatter.19.cloned.1.call-update) | async-done | bytes 524304 | tf_op jit(solution)/shard_map/reduce_scatter | solution.py:319
  1111.7 65.4 %all-reduce = (f32[2048]{0:T(1024)}, f32[2048]{0:T(1024)}) all-reduce(f32[2048]{0:T(1024)S(1)} %get-tuple-element.238, f32[2048]{0:T(1024)S(1)} %get-tuple-element.236), channel_id=1, replica_groups=mesh['fsdp'=16,'ctx'=2,'tp'=4] {'fsdp','ctx','tp'}, use_global_device_ids=true, to_apply=%region_19.20 | all-reduce | flops 4096 | bytes 32768 | tf_op jit(solution)/shard_map/psum | solution.py:330
  1179.6 12.6 reduce-scatter.29.cloned.1.call-done
  1193.8 82.6 %reduce-scatter.25.cloned.1.call-done = bf16[64,864]{1,0:T(8,128)(2,1)} async-done(((bf16[2048,864]{1,0:T(8,128)(2,1)}), bf16[64,864]{1,0:T(8,128)(2,1)}) %reduce-scatter.25.cloned.1.call-update) | async-done | bytes 110608 | tf_op jit(solution)/shard_map/reduce_scatter | solution.py:338
  1278.0 82.9 %reduce-scatter.27.cloned.1.call-done = bf16[64,864]{1,0:T(8,128)(2,1)} async-done(((bf16[2048,864]{1,0:T(8,128)(2,1)}), bf16[64,864]{1,0:T(8,128)(2,1)}) %reduce-scatter.27.cloned.1.call-update) | async-done | bytes 110608 | tf_op jit(solution)/shard_map/reduce_scatter | solution.py:341
  (259 shorter events, 217.2 us)
Async XLA Ops:
  7.2 39.0 %all-gather.15.cloned.1.call-start = ((), (), s32[]{:S(2)}) async-start(), calls=%async_computation.12 | async-start | bytes 2621440 | tf_op jit(solution)/shard_map/all_gather | solution.py:143
  12.0 80.9 %all-gather.19.cloned.1.call-start = ((), (), s32[]{:S(2)}) async-start(), calls=%async_computation.14 | async-start | bytes 2162688 | tf_op jit(solution)/shard_map/all_gather | solution.py:132
  12.8 125.7 %all-gather.21.cloned.1.call-start = ((), (), s32[]{:S(2)}) async-start(), calls=%async_computation.15 | async-start | bytes 2162688 | tf_op jit(solution)/shard_map/all_gather | solution.py:133
  13.5 172.2 %all-gather.23.cloned.1.call-start = ((), (), s32[]{:S(2)}) async-start(), calls=%async_computation.16 | async-start | bytes 3784704 | tf_op jit(solution)/shard_map/all_gather | solution.py:134
  14.1 190.7 %all-gather.37.cloned.1.call-start = ((), (), s32[]{:S(2)}) async-start(), calls=%async_computation.35 | async-start | bytes 2654208 | tf_op jit(solution)/shard_map/all_gather | solution.py:16
  192.5 61.6 %all-gather.17.cloned.1.call-start = ((), (), s32[]{:S(2)}) async-start(), calls=%async_computation.13 | async-start | bytes 3784704 | tf_op jit(solution)/shard_map/all_gather | solution.py:135
  193.1 108.5 %all-gather.25.cloned.1.call-start = ((), (), s32[]{:S(2)}) async-start(), calls=%async_computation.17 | async-start | bytes 3784704 | tf_op jit(solution)/shard_map/all_gather | solution.py:136
  193.8 160.1 %reduce-scatter.13.cloned.1.call-start = ((), (), s32[]{:S(2)}) async-start(), calls=%async_computation.18 | async-start | bytes 5242880 | tf_op jit(solution)/shard_map/reduce_scatter | solution.py:190
  308.0 94.4 %all-gather.29.cloned.1.call-start = ((), (), s32[]{:S(2)}) async-start(), calls=%async_computation.20 | async-start | bytes 3784704 | tf_op jit(solution)/shard_map/all_gather | solution.py:137
  308.8 125.6 %all-gather.27.cloned.1.call-start = ((), (), s32[]{:S(2)}) async-start(), calls=%async_computation.19 | async-start | bytes 2621440 | tf_op jit(solution)/shard_map/all_gather | solution.py:198
  356.7 126.6 %all-gather.33.cloned.1.call-start = ((), (), s32[]{:S(2)}) async-start(), calls=%async_computation.22 | async-start | bytes 3784704 | tf_op jit(solution)/shard_map/all_gather | solution.py:139
  357.4 173.4 %all-gather.31.cloned.1.call-start = ((), (), s32[]{:S(2)}) async-start(), calls=%async_computation.21 | async-start | bytes 3784704 | tf_op jit(solution)/shard_map/all_gather | solution.py:138
  358.0 233.9 %reduce-scatter.17.cloned.1.call-start = ((), (), s32[]{:S(2)}) async-start(), calls=%async_computation.24 | async-start | bytes 5242880 | tf_op jit(solution)/shard_map/reduce_scatter | solution.py:223
  545.9 77.6 %reduce-scatter.15.cloned.1.call-start = ((), (), s32[]{:S(2)}) async-start(), calls=%async_computation.23 | async-start | bytes 2621440 | tf_op jit(solution)/shard_map/reduce_scatter | solution.py:206
  552.1 107.7 %all-gather.35.cloned.1.call-start = ((), (), s32[]{:S(2)}) async-start(), calls=%async_computation.25 | async-start | bytes 2621440 | tf_op jit(solution)/shard_map/all_gather | solution.py:233
  629.1 114.4 %reduce-scatter.31.cloned.1.call-start = ((), (), s32[]{:S(2)}) async-start(), calls=%async_computation.32 | async-start | bytes 3784704 | tf_op jit(solution)/shard_map/reduce_scatter | solution.py:347
  635.0 192.6 %reduce-scatter.33.cloned.1.call-start = ((), (), s32[]{:S(2)}) async-start(), calls=%async_computation.33 | async-start | bytes 3784704 | tf_op jit(solution)/shard_map/reduce_scatter | solution.py:350
  641.9 270.2 %reduce-scatter.35.cloned.1.call-start = ((), (), s32[]{:S(2)}) async-start(), calls=%async_computation.34 | async-start | bytes 3784704 | tf_op jit(solution)/shard_map/reduce_scatter | solution.py:353
  650.6 343.3 %reduce-scatter.23.cloned.1.call-start = ((), (), s32[]{:S(2)}) async-start(), calls=%async_computation.28 | async-start | bytes 2162688 | tf_op jit(solution)/shard_map/reduce_scatter | solution.py:335
  689.1 386.4 %reduce-scatter.21.cloned.1.call-start = ((), (), s32[]{:S(2)}) async-start(), calls=%async_computation.27 | async-start | bytes 2162688 | tf_op jit(solution)/shard_map/reduce_scatter | solution.py:332
  696.2 412.5 %reduce-scatter.19.cloned.1.call-start = ((), (), s32[]{:S(2)}) async-start(), calls=%async_computation.26 | async-start | bytes 2621440 | tf_op jit(solution)/shard_map/reduce_scatter | solution.py:319
  710.6 481.7 %reduce-scatter.29.cloned.1.call-start = ((), (), s32[]{:S(2)}) async-start(), calls=%async_computation.31 | async-start | bytes 3784704 | tf_op jit(solution)/shard_map/reduce_scatter | solution.py:344
  717.5 558.9 %reduce-scatter.25.cloned.1.call-start = ((), (), s32[]{:S(2)}) async-start(), calls=%async_computation.29 | async-start | bytes 3784704 | tf_op jit(solution)/shard_map/reduce_scatter | solution.py:338
  723.7 637.2 %reduce-scatter.27.cloned.1.call-start = ((), (), s32[]{:S(2)}) async-start(), calls=%async_computation.30 | async-start | bytes 3784704 | tf_op jit(solution)/shard_map/reduce_scatter | solution.py:341
  (47 other events, 1244.6 us)
Sparse Core Ops, SparseCore 0:
  12.1 34.0 all-gather.14
  48.5 44.3 all-gather.18
  95.2 43.2 all-gather.20
  140.5 45.1 all-gather.22
  192.6 12.0 all-gather.36
  206.9 47.2 all-gather.16
  256.4 45.1 all-gather.24
  308.2 45.7 reduce-scatter.12
  356.5 45.9 all-gather.28
  404.6 29.7 all-gather.26
  436.9 46.3 all-gather.32
  485.6 45.1 all-gather.30
  546.1 45.7 reduce-scatter.16
  594.1 29.3 reduce-scatter.14
  629.2 30.4 all-gather.34
  663.7 79.6 reduce-scatter.30
  747.0 80.5 reduce-scatter.32
  831.5 80.5 reduce-scatter.34
  915.7 78.2 reduce-scatter.22
  997.3 78.2 reduce-scatter.20
  1078.0 30.5 reduce-scatter.18
  1112.7 79.4 reduce-scatter.28
  1195.9 80.4 reduce-scatter.24
  1280.4 80.4 reduce-scatter.26
where the time goes:
time: 1380 us; the launch traced here: 1370 us
  waiting for transfers between devices  1080 us (78%)
  matrix products  135 us (10%)
  blocking collectives  72.6 us (5%)
  other arithmetic  44.7 us (3%)
  local copies, waits for them, and re-layouts  16.9 us (1%)
  between operations  15.9 us (1%)
    reduce_scatter x1, waiting for transfers between devices, on_device(): lax.psum_scatter(down_part.astype(jnp.bfloat16), ('fsdp', 'ctx'), scatter...  82.9 us
    reduce_scatter x1, waiting for transfers between devices, on_device(): lax.psum_scatter(swish_part.astype(jnp.bfloat16), ('fsdp', 'ctx'), scatte...  82.9 us
    reduce_scatter x1, waiting for transfers between devices, on_device(): lax.psum_scatter(value_part.astype(jnp.bfloat16), ('fsdp', 'ctx'), scatte...  82.6 us
    reduce_scatter x1, waiting for transfers between devices, on_device(): lax.psum_scatter(up_part.astype(jnp.bfloat16), ('fsdp', 'ctx'), scatter_d...  82.5 us
    reduce_scatter x1, waiting for transfers between devices, on_device(): lax.psum_scatter(key_part.astype(jnp.bfloat16), ('fsdp', 'ctx'), scatter_...  80.2 us
    reduce_scatter x1, waiting for transfers between devices, on_device(): lax.psum_scatter(query_part.astype(jnp.bfloat16), ('fsdp', 'ctx'), scatte...  80.1 us
    psum x1, blocking collectives, on_device(): lax.psum((attn_gain_part, mlp_gain_part), ('fsdp', 'ctx', 'tp'))  65.4 us
    all_gather x1, waiting for transfers between devices, on_device(): lax.all_gather(query_weight, ('fsdp', 'ctx'), axis=0, tiled=True)  46.7 us
  transfers between devices with their start and end apart: 24, of which 24 were waited for; matrix products, arithmetic and copies ran while one was open for 11% of the time, Pallas kernels for 0%

commit v1 on v0

v1 whole, which is shorter than its diff:
```python
import functools

import jax
import jax.numpy as jnp
from jax import lax
from jax.experimental import pallas as pl
from jax.experimental.pallas import tpu as pltpu
from jax.sharding import PartitionSpec as P

D = 2048
KDIM = 256
VDIM = 432
SEQ = 1024
HALF = 512
SIZES = (256, 256, 432, 432, 432, 432, 432, 432)
STARTS = (0, 256, 512, 944, 1376, 1808, 2240, 2672)
ROWS = 3104
EPSILON = 1e-05
MESH = pl.DeviceIdType.MESH
BF = jnp.bfloat16
F32 = jnp.float32


def even(rows):
    return rows // 32 * 16


class Net:
    def __init__(self, send, recv):
        group = lax.axis_index("fsdp")
        self.c = lax.axis_index("ctx")
        self.t = lax.axis_index("tp")
        self.x = group // 4
        self.z = group % 4
        self.send, self.recv, self.used = send, recv, 0

    def dev(self, dx=0, dz=0, dt=0, dc=0):
        x, z, t = ((at + d + 4) % 4 if d else at for at, d in ((self.x, dx), (self.z, dz), (self.t, dt)))
        c = 1 - self.c if dc else self.c
        return (x * 4 + z, c, t)

    def greet(self, hops):
        barrier = pltpu.get_barrier_semaphore()
        for hop in hops:
            pl.semaphore_signal(barrier, inc=1, device_id=self.dev(**hop), device_id_type=MESH)
        pl.semaphore_wait(barrier, len(hops))

    def copy(self, src, dst, **hop):
        at = self.used
        self.used += 1
        return pltpu.make_async_remote_copy(
            src_ref=src,
            dst_ref=dst,
            send_sem=self.send.at[at],
            recv_sem=self.recv.at[at],
            device_id=self.dev(**hop),
            device_id_type=MESH,
        )


XZ_HOPS = (dict(dx=1), dict(dx=-1), dict(dz=1), dict(dz=-1))
Y_HOPS = (dict(dt=1), dict(dt=-1), dict(dc=1))


def lanes(piece):
    return pl.ds(pl.multiple_of(piece * 128, 128), 128)


def ring_views(net, axis):
    x, z = net.x, net.z
    if axis == "x":
        first = lambda ref, d, rows: ref.at[(x + d + 4) % 4, rows, lanes(z)]
        second = lambda ref, d, rows: ref.at[:, rows, lanes((z + d + 4) % 4)]
        return first, second, "dx", "dz"
    first = lambda ref, d, rows: ref.at[x, rows, lanes((z + d + 4) % 4)]
    second = lambda ref, d, rows: ref.at[(x + d + 4) % 4, rows, :]
    return first, second, "dz", "dx"


def gather_weights(net, ref, start, stop):
    cut = start + even(stop - start)
    plans = []
    for axis, lo, hi in (("z", start, cut), ("x", cut, stop)):
        mid = lo + even(hi - lo)
        whole, head, tail = pl.ds(lo, hi - lo), pl.ds(lo, mid - lo), pl.ds(mid, hi - mid)
        first, second, hop_a, hop_b = ring_views(net, axis)
        plan = []
        for view, hop in ((first, hop_a), (second, hop_b)):
            mine = view(ref, 0, whole)
            plan.append(
                (
                    net.copy(mine, mine, **{hop: 1}),
                    net.copy(mine, mine, **{hop: -1}),
                    net.copy(view(ref, -1, head), view(ref, -1, head), **{hop: 1}),
                    net.copy(view(ref, 1, tail), view(ref, 1, tail), **{hop: -1}),
                )
            )
        plans.append(plan)

    def near(phase):
        for plan in plans:
            plan[phase][0].start()
            plan[phase][1].start()

    def far(phase):
        for k in (0, 1):
            for plan in plans:
                plan[phase][k].wait_recv()
                plan[phase][2 + k].start()

    def land(phase):
        for plan in plans:
            plan[phase][2].wait_recv()
            plan[phase][3].wait_recv()

    def done():
        land(1)
        for plan in plans:
            for phase in plan:
                for copy in phase:
                    copy.wait_send()

    return [
        lambda: near(0),
        lambda: far(0),
        lambda: (land(0), near(1)),
        lambda: far(1),
        done,
    ]


def add_rows(refs, out, count):
    step = 16

    def body(i, carry):
        at = pl.ds(pl.multiple_of(i * step, step), step)
        total = refs[0](at).astype(F32)
        for ref in refs[1:]:
            total = total + ref(at).astype(F32)
        out(at, total)
        return carry

    lax.fori_loop(0, count // step, body, 0)


def scatter_shapes(rows):
    shapes = []
    cut = even(rows)
    for axis, count in (("z", cut), ("x", rows - cut)):
        head = even(count)
        for slab in ((4, 128), (1, 128)) if axis == "z" else ((1, 512), (1, 128)):
            for n in (head, count - head, count, count):
                shape = (n, slab[1]) if slab[0] == 1 else (slab[0], n, slab[1])
                shapes.append(pltpu.VMEM(shape, BF))
    return shapes


def scatter_weights(net, ref, start, stop, bufs, out):
    cut = start + even(stop - start)
    plans = []
    bufs = list(bufs)
    for axis, lo, hi in (("z", start, cut), ("x", cut, stop)):
        mid = lo + even(hi - lo)
        parts = (lo, mid - lo), (mid, hi - mid), (lo, hi - lo)
        head, tail, whole = (pl.ds(*part) for part in parts)
        far_view, near_view, hop_a, hop_b = ring_views(net, axis)
        plan = []
        if axis == "z":
            wide = lambda r, d, rows: r.at[:, rows, lanes((net.z + d + 4) % 4)]
            thin = lambda r, d, rows: r.at[(net.x + d + 4) % 4, rows, lanes(net.z)]
        else:
            wide = lambda r, d, rows: r.at[(net.x + d + 4) % 4, rows, :]
            thin = lambda r, d, rows: r.at[net.x, rows, lanes((net.z + d + 4) % 4)]
        for view, hop in ((wide, hop_a), (thin, hop_b)):
            fa, fb, ma, mb = bufs[:4]
            bufs = bufs[4:]
            plan.append(
                dict(
                    view=view,
                    bufs=(fa, fb, ma, mb),
                    copies=(
                        net.copy(view(ref, 2, head), fa, **{hop: 1}),
                        net.copy(view(ref, 2, tail), fb, **{hop: -1}),
                        net.copy(view(ref, 1, whole), ma, **{hop: 1}),
                        net.copy(view(ref, -1, whole), mb, **{hop: -1}),
                    ),
                )
            )
        plans.append((plan, parts))

    def at_rows(view, d, lo):
        def read(at):
            return view(ref, d, pl.ds(lo + at.start, at.size))[...]

        def write(at, value):
            view(ref, d, pl.ds(lo + at.start, at.size))[...] = value.astype(BF)

        return read, write

    def buf_rows(buf):
        if len(buf.shape) == 3:
            return lambda at: buf[:, at, :]
        return lambda at: buf[at, :]

    def far(phase):
        for plan, _ in plans:
            plan[phase]["copies"][0].start()
            plan[phase]["copies"][1].start()

    def near(phase):
        for k, d in ((0, 1), (1, -1)):
            for plan, parts in plans:
                step = plan[phase]
                lo, count = parts[k]
                step["copies"][k].wait_recv()
                read, write = at_rows(step["view"], d, lo)
                add_rows((read, buf_rows(step["bufs"][k])), write, count)
                step["copies"][2 + k].start()

    def total(phase, last):
        for plan, parts in plans:
            step = plan[phase]
            lo, count = parts[2]
            step["copies"][2].wait_recv()
            step["copies"][3].wait_recv()
            read, write = at_rows(step["view"], 0, lo)
            if last:
                write = lambda at, value, lo=lo: out(pl.ds(lo + at.start, at.size), value)
            add_rows((read, buf_rows(step["bufs"][2]), buf_rows(step["bufs"][3])), write, count)

    def done():
        total(1, True)
        for plan, _ in plans:
            for step in plan:
                for copy in step["copies"]:
                    copy.wait_send()

    return [
        lambda: far(0),
        lambda: near(0),
        lambda: (total(0, False), far(1)),
        lambda: near(1),
        done,
    ]


def gather_rows(net, ref):
    def block(c, t, lo=0, n=128):
        return ref.at[pl.ds(pl.multiple_of(c * 512 + t * 128 + lo, 16), n), :]

    c, t = net.c, net.t
    before, after, across = (t + 3) % 4, (t + 1) % 4, (t + 2) % 4
    own = block(c, t)
    up = net.copy(own, own, dt=1)
    down = net.copy(own, own, dt=-1)
    side = net.copy(own, own, dc=1)
    fore = net.copy(block(c, before, 0, 64), block(c, before, 0, 64), dt=1)
    back = net.copy(block(c, after, 64, 64), block(c, after, 64, 64), dt=-1)
    over = [
        net.copy(block(c, before), block(c, before), dc=1),
        net.copy(block(c, after), block(c, after), dc=1),
        net.copy(block(c, across, 0, 64), block(c, across, 0, 64), dc=1),
        net.copy(block(c, across, 64, 64), block(c, across, 64, 64), dc=1),
    ]

    def start():
        up.start()
        down.start()
        side.start()

    def forward():
        up.wait_recv()
        fore.start()
        over[0].start()
        down.wait_recv()
        back.start()
        over[1].start()

    def finish():
        fore.wait_recv()
        over[2].start()
        back.wait_recv()
        over[3].start()
        side.wait_recv()
        for copy in over:
            copy.wait_recv()
        for copy in (up, down, side, fore, back, *over):
            copy.wait_send()

    return [start, forward, finish]


ROW_BUFS = [
    pltpu.VMEM((512, D), BF),
    pltpu.VMEM((64, D), BF),
    pltpu.VMEM((64, D), BF),
    pltpu.VMEM((128, D), BF),
    pltpu.VMEM((128, D), BF),
]


def scatter_rows(net, ref, bufs, out):
    c, t = net.c, net.t
    other, far_a, far_b, near_a, near_b = bufs
    side = net.copy(ref.at[pl.ds(pl.multiple_of((1 - c) * 512, 512), 512), :], other, dc=1)

    def row(d, lo=0):
        return c * 512 + (t + d + 4) % 4 * 128 + lo

    def block(d, lo=0, n=128):
        return ref.at[pl.ds(pl.multiple_of(row(d, lo), 16), n), :]

    copies = (
        net.copy(block(2, 0, 64), far_a, dt=1),
        net.copy(block(2, 64, 64), far_b, dt=-1),
        net.copy(block(1), near_a, dt=1),
        net.copy(block(-1), near_b, dt=-1),
    )

    def read(source, base):
        return lambda at: source[pl.ds(pl.multiple_of(base + at.start, 16), at.size), :]

    def write(base):
        def store(at, value):
            ref[pl.ds(pl.multiple_of(base + at.start, 16), at.size), :] = value.astype(BF)

        return store

    def other_row(d, lo=0):
        return (t + d + 4) % 4 * 128 + lo

    def start():
        side.start()

    def far():
        side.wait_recv()
        for d, lo, k in ((2, 0, 0), (2, 64, 1)):
            add_rows((read(ref, row(d, lo)), read(other, other_row(d, lo))), write(row(d, lo)), 64)
            copies[k].start()
        for d in (1, -1, 0):
            add_rows((read(ref, row(d)), read(other, other_row(d))), write(row(d)), 128)

    def near():
        for k, d, lo, buf in ((0, 1, 0, far_a), (1, -1, 64, far_b)):
            copies[k].wait_recv()
            add_rows((read(ref, row(d, lo)), read(buf, 0)), write(row(d, lo)), 64)
            copies[2 + k].start()

    def finish():
        copies[2].wait_recv()
        copies[3].wait_recv()
        add_rows((read(ref, row(0)), read(near_a, 0), read(near_b, 0)), out, 128)
        for copy in (side, *copies):
            copy.wait_send()

    return [start, far, near, finish]


def call(kernel, outs, ins, scratch, copies, cid):
    any_spec = pl.BlockSpec(memory_space=pl.ANY)
    vmem_spec = pl.BlockSpec(memory_space=pltpu.VMEM)
    return pl.pallas_call(
        kernel,
        out_shape=[shape for shape, _ in outs],
        in_specs=[vmem_spec if v else any_spec for _, v in ins],
        out_specs=[vmem_spec if v else any_spec for _, v in outs],
        scratch_shapes=list(scratch)
        + [pltpu.SemaphoreType.DMA((copies,)), pltpu.SemaphoreType.DMA((copies,)), pltpu.SemaphoreType.DMA((40,))],
        compiler_params=pltpu.CompilerParams(
            collective_id=cid, has_side_effects=True, vmem_limit_bytes=56 * 2**20
        ),
    )(*[array for array, _ in ins])


def weights_in(piece, cid):
    def kernel(piece_ref, out_ref, send, recv, local):
        net = Net(send, recv)
        own = pltpu.make_async_copy(piece_ref, out_ref.at[net.x, :, lanes(net.z)], local.at[0])
        own.start()
        net.greet(XZ_HOPS)
        own.wait()
        for stage in gather_weights(net, out_ref, 0, ROWS):
            stage()

    (out,) = call(
        kernel, [(jax.ShapeDtypeStruct((4, ROWS, 512), BF), False)], [(piece, False)], [], 16, cid
    )
    return out


def grads_out(parts, cid):
    def kernel(*refs):
        parts_refs, out_ref, total = refs[:8], refs[8], refs[9]
        bufs, (send, recv, local) = refs[10:-3], refs[-3:]
        net = Net(send, recv)
        loads = []
        for k, ref in enumerate(parts_refs):
            for x in range(4):
                loads.append(
                    pltpu.make_async_copy(
                        ref.at[:, pl.ds(x * 512, 512)],
                        total.at[x, pl.ds(STARTS[k], SIZES[k]), :],
                        local.at[4 * k + x],
                    )
                )
        for load in loads:
            load.start()
        net.greet(XZ_HOPS)
        for load in loads:
            load.wait()

        def out(at, value):
            out_ref[at, :] = value

        for stage in scatter_weights(net, total, 0, ROWS, bufs, out):
            stage()

    (out,) = call(
        kernel,
        [(jax.ShapeDtypeStruct((ROWS, 128), F32), True)],
        [(part, False) for part in parts],
        [pltpu.VMEM((4, ROWS, 512), BF)] + scatter_shapes(ROWS),
        16,
        cid,
    )
    return out


def rows_in(own, cid):
    def kernel(own_ref, out_ref, send, recv, local):
        net = Net(send, recv)
        at = pl.ds(pl.multiple_of(net.c * 512 + net.t * 128, 128), 128)
        load = pltpu.make_async_copy(own_ref, out_ref.at[at, :], local.at[0])
        load.start()
        net.greet(Y_HOPS)
        load.wait()
        for stage in gather_rows(net, out_ref):
            stage()

    (out,) = call(kernel, [(jax.ShapeDtypeStruct((SEQ, D), BF), False)], [(own, False)], [], 9, cid)
    return out


def rows_out(part, cid):
    def kernel(part_ref, out_ref, total, *rest):
        bufs, (send, recv, local) = rest[:5], rest[5:]
        net = Net(send, recv)
        load = pltpu.make_async_copy(part_ref, total, local.at[0])
        load.start()
        net.greet(Y_HOPS)
        load.wait()

        def out(at, value):
            out_ref[at, :] = value

        for stage in scatter_rows(net, total, bufs, out):
            stage()

    (out,) = call(
        kernel,
        [(jax.ShapeDtypeStruct((128, D), F32), True)],
        [(part, False)],
        [pltpu.VMEM((SEQ, D), BF)] + ROW_BUFS,
        5,
        cid,
    )
    return out


def dot(a, b, dims):
    return lax.dot_general(a, b, (dims, ((), ())), preferred_element_type=F32)


NN = ((1,), (0,))
NT = ((1,), (1,))
TN = ((0,), (0,))


def layer_norm(rows_in, gain):
    centre = jnp.mean(rows_in, axis=-1, keepdims=True)
    centred = rows_in - centre
    spread = jnp.mean(centred * centred, axis=-1, keepdims=True)
    return centred * lax.rsqrt(spread + EPSILON) * gain


def group_norm(values_in):
    centre = jnp.mean(values_in, axis=-1, keepdims=True)
    centred = values_in - centre
    spread = jnp.mean(centred * centred, axis=-1, keepdims=True)
    return centred * lax.rsqrt(spread + EPSILON)


def rotate(field, cosine, sine):
    former, latter = field[:, :128], field[:, 128:]
    return jnp.concatenate([former * cosine - latter * sine, former * sine + latter * cosine], axis=1)


def swap_cores(array):
    return lax.ppermute(array, "ctx", [(0, 1), (1, 0)])


def on_device(
    inputs,
    seq_lengths,
    carried_state,
    attn_gain,
    query_weight,
    key_weight,
    value_weight,
    swish_weight,
    out_weight,
    mlp_gain,
    gate_weight,
    up_weight,
    down_weight,
    output_grad,
):
    core = lax.axis_index("ctx")
    head = lax.axis_index("tp") * 2 + core

    def for_core(which):
        parts = []
        for k, weight in enumerate(
            (query_weight, key_weight, value_weight, swish_weight, out_weight, gate_weight, up_weight, down_weight)
        ):
            n = SIZES[k]
            if k in (4, 7):
                parts.append(lax.dynamic_slice_in_dim(weight, which * n, n, 0))
            else:
                parts.append(lax.dynamic_slice_in_dim(weight, which * n, n, 1).T)
        return jnp.concatenate(parts, axis=0)

    mine, got = for_core(core), swap_cores(for_core(1 - core))
    piece = jnp.where(core == 0, jnp.concatenate([mine, got], axis=1), jnp.concatenate([got, mine], axis=1))
    weights = weights_in(piece, 1)
    weights = weights.transpose(1, 0, 2).reshape(ROWS, D)
    w_query, w_key, w_value, w_swish, w_out, w_gate, w_up, w_down = (
        weights[s : s + n] for s, n in zip(STARTS, SIZES)
    )
    position = jnp.arange(SEQ, dtype=jnp.int32)
    row_mask = (position < seq_lengths[0]).astype(F32)[:, None]
    frequency = jnp.power(10000.0, -jnp.arange(128).astype(F32) / 128)
    angles = position.astype(F32)[:, None] * frequency[None, :]
    cosine, sine = jnp.cos(angles), jnp.sin(angles)
    decay = -jnp.power(2.0, 5.0 - head.astype(F32)) / SEQ
    local_pos = jnp.arange(HALF).astype(F32)
    tail_fac = jnp.exp((HALF - 1.0 - local_pos) * decay)[:, None]
    head_fac = jnp.exp((local_pos + 1.0) * decay)[:, None]
    span = jnp.exp(HALF * decay)
    distance = local_pos[:, None] - local_pos[None, :]
    decay_mask = jnp.where(distance >= 0.0, jnp.exp(jnp.maximum(distance, 0.0) * decay), 0.0)
    carried = lax.dynamic_index_in_dim(carried_state[0], core, 0, keepdims=False)

    inputs_wide = inputs.astype(F32)
    rows_one = rows_in(layer_norm(inputs_wide, attn_gain).astype(BF), 2)
    queries = rotate(dot(rows_one, w_query, NT), cosine, sine).astype(BF)
    keys_rot = rotate(dot(rows_one, w_key, NT), cosine, sine).astype(BF)
    values_kept = (dot(rows_one, w_value, NT) * row_mask).astype(BF)
    swish_raw = dot(rows_one, w_swish, NT)
    stretch = lambda a: (a[:HALF], a[HALF:])
    qs, ks, vs = stretch(queries), stretch(keys_rot), stretch(values_kept)
    mixing = [(dot(q, k, NT) * decay_mask).astype(BF) for q, k in zip(qs, ks)]
    local_state = dot((ks[0] * tail_fac).astype(BF), vs[0], TN)
    prior = [carried.astype(BF), (span * carried + local_state).astype(BF)]
    retained = jnp.concatenate(
        [dot(m, v, NN) + dot(q, p, NN) * head_fac for m, v, q, p in zip(mixing, vs, qs, prior)], axis=0
    )

    def gate_piece(swish_in, retained_in):
        return row_mask * jax.nn.silu(swish_in) * group_norm(retained_in)

    mixed = gate_piece(swish_raw, retained).astype(BF)
    hidden = inputs_wide + rows_out(dot(mixed, w_out, NN).astype(BF), 3)
    rows_two = rows_in(layer_norm(hidden, mlp_gain).astype(BF), 4)
    gate_pre = dot(rows_two, w_gate, NT)
    up_pre = dot(rows_two, w_up, NT)

    def mlp_piece(gate_in, up_in):
        return jax.nn.gelu(gate_in, approximate=False) * up_in

    activated = mlp_piece(gate_pre, up_pre).astype(BF)
    outputs = (hidden + rows_out(dot(activated, w_down, NN).astype(BF), 5)).astype(BF)
    grad_all = lax.all_gather(output_grad, "ctx", axis=0, tiled=True)
    grad_own = lax.dynamic_slice_in_dim(output_grad, lax.axis_index("tp") * 128, 128, 0).astype(F32)
    down_part = dot(activated, grad_all, TN)
    grad_act = dot(grad_all, w_down, NT)
    _, mlp_pull = jax.vjp(mlp_piece, gate_pre, up_pre)
    grad_gate, grad_up = (g.astype(BF) for g in mlp_pull(grad_act))
    gate_part = dot(grad_gate, rows_two, TN)
    up_part = dot(grad_up, rows_two, TN)
    grad_norm_two = rows_out((dot(grad_gate, w_gate, NN) + dot(grad_up, w_up, NN)).astype(BF), 6)
    _, norm_two_pull = jax.vjp(layer_norm, hidden, mlp_gain)
    grad_hidden_norm, mlp_gain_part = norm_two_pull(grad_norm_two)
    grad_hidden = grad_own + grad_hidden_norm
    mid_rows = rows_in(grad_hidden.astype(BF), 7)
    out_part = dot(mixed, mid_rows, TN)
    grad_mixed = dot(mid_rows, w_out, NT)
    _, gate_pull = jax.vjp(gate_piece, swish_raw, retained)
    grad_swish, grad_retained = (g.astype(BF) for g in gate_pull(grad_mixed))
    rs = stretch(grad_retained)
    grad_local = dot((qs[1] * head_fac).astype(BF), rs[1], TN).astype(BF)
    gq, gk, gv = [], [], []
    for at in (0, 1):
        grad_scores = (dot(rs[at], vs[at], NT) * decay_mask).astype(BF)
        gq.append(dot(grad_scores, ks[at], NN) + dot(rs[at], prior[at], NT) * head_fac)
        gk.append(dot(grad_scores, qs[at], TN))
        gv.append(dot(mixing[at], rs[at], TN))
    gk[0] = gk[0] + dot(vs[0], grad_local, NT) * tail_fac
    gv[0] = gv[0] + dot(ks[0], grad_local, NN) * tail_fac
    grad_query = rotate(jnp.concatenate(gq, axis=0), cosine, -sine).astype(BF)
    grad_key = rotate(jnp.concatenate(gk, axis=0), cosine, -sine).astype(BF)
    grad_value = (jnp.concatenate(gv, axis=0) * row_mask).astype(BF)
    four = (grad_query, grad_key, grad_value, grad_swish)
    sums = [dot(g, rows_one, TN) for g in four]
    total_rows = sum(dot(g, w, NN) for g, w in zip(four, (w_query, w_key, w_value, w_swish)))
    grad_norm_one = rows_out(total_rows.astype(BF), 8)
    _, norm_one_pull = jax.vjp(layer_norm, inputs_wide, attn_gain)
    grad_inputs_norm, attn_gain_part = norm_one_pull(grad_norm_one)
    input_grad = grad_hidden + grad_inputs_norm
    attn_gain_grad, mlp_gain_grad = lax.psum((attn_gain_part, mlp_gain_part), ("fsdp", "ctx", "tp"))

    summed = grads_out([part.astype(BF) for part in (*sums, out_part, gate_part, up_part, down_part)], 9)
    left, right = summed[:, :64], summed[:, 64:]
    mine = jnp.where(core == 0, left, right)
    got = swap_cores(jnp.where(core == 0, right, left))
    first, second = jnp.where(core == 0, mine, got), jnp.where(core == 0, got, mine)
    grads = []
    for k, (s, n) in enumerate(zip(STARTS, SIZES)):
        both = jnp.concatenate([first[s : s + n], second[s : s + n]], axis=0)
        grads.append(both if k in (4, 7) else both.T)
    return (
        outputs,
        input_grad,
        attn_gain_grad,
        grads[0],
        grads[1],
        grads[2],
        grads[3],
        grads[4],
        mlp_gain_grad,
        grads[5],
        grads[6],
        grads[7],
    )


def solution(mesh):
    placed = (
        P(("fsdp", "ctx", "tp"), None),
        P("fsdp"),
        P("fsdp", "tp", None, None),
        P(),
        P(("fsdp", "ctx"), "tp"),
        P(("fsdp", "ctx"), "tp"),
        P(("fsdp", "ctx"), "tp"),
        P(("fsdp", "ctx"), "tp"),
        P("tp", ("fsdp", "ctx")),
        P(),
        P(("fsdp", "ctx"), "tp"),
        P(("fsdp", "ctx"), "tp"),
        P("tp", ("fsdp", "ctx")),
        P(("fsdp", "ctx"), None),
    )
    return jax.shard_map(
        on_device,
        mesh=mesh,
        in_specs=placed,
        out_specs=(
            P(("fsdp", "ctx", "tp"), None),
            P(("fsdp", "ctx", "tp"), None),
            P(),
            P(("fsdp", "ctx"), "tp"),
            P(("fsdp", "ctx"), "tp"),
            P(("fsdp", "ctx"), "tp"),
            P(("fsdp", "ctx"), "tp"),
            P("tp", ("fsdp", "ctx")),
            P(),
            P(("fsdp", "ctx"), "tp"),
            P(("fsdp", "ctx"), "tp"),
            P("tp", ("fsdp", "ctx")),
        ),
        check_vma=False,
    )
```

time: 1380 us -> 707 us (0.51)
  waiting for transfers between devices: 1080 us -> 0.69 us
  Pallas kernels: 0 us -> 435 us
  local copies, waits for them, and re-layouts: 16.9 us -> 43.2 us
  matrix products: 135 us -> 114 us
  other arithmetic: 44.7 us -> 25.9 us
    reduce_scatter x12 -> x0, waiting for transfers between devices: 663 us -> none  [the longest x1 82.9 us: on_device(): lax.psum_scatter(down_part.astype(jnp.bfloat16), ('fsdp', 'ctx'), scatter...]
    pallas_call x0 -> x9, Pallas kernels: none -> 435 us  [call(): pl.pallas_call(kernel, out_shape=[shape for shape, _ in outs], in_specs=[...]
    all_gather x12 -> x1, waiting for transfers between devices: 414 us -> 0.01 us  [on_device(): grad_all = lax.all_gather(output_grad, 'ctx', axis=0, tiled=True)]
    dot_general x36 -> x44, matrix products: 135 us -> 114 us  [dot(): return lax.dot_general(a, b, (dims, ((), ())), preferred_element_type=F32)]
    convert_element_type x19 -> x7, other arithmetic: 19.8 us -> 4.4 us  [the longest x1 2.02 us: on_device(): mid_rows = rows_in(grad_hidden.astype(BF), 7)]
  transfers between devices with their start and end apart: 24 -> 3, of which waited for: 24 -> 0; matrix products, arithmetic and copies ran while one was open for 11% -> 10% of each run, Pallas kernels for 0% -> 36%
where the time goes in v1:
time: 707 us; the launch traced here: 705 us
  Pallas kernels  435 us (62%)
  matrix products  114 us (16%)
  blocking collectives  65.8 us (9%)
  local copies, waits for them, and re-layouts  43.2 us (6%)
  other arithmetic  25.9 us (4%)
  between operations  16.3 us (2%)
    pallas_call x9, Pallas kernels, call(): pl.pallas_call(kernel, out_shape=[shape for shape, _ in outs], in_specs=[...  435 us
    dot_general x44, matrix products, dot(): return lax.dot_general(a, b, (dims, ((), ())), preferred_element_type=F32)  114 us
    psum x1, blocking collectives, on_device(): lax.psum((attn_gain_part, mlp_gain_part), ('fsdp', 'ctx', 'tp'))  65.8 us
    unnamed x174, local copies, waits for them, and re-layouts  26.4 us
  transfers between devices with their start and end apart: 3, of which 0 were waited for; matrix products, arithmetic and copies ran while one was open for 10% of the time, Pallas kernels for 36%

profile of v1, /device:TPU:1, one launch (start us, length us, event | category | flops | bytes accessed | tf_op | source)
XLA Modules:
  0.0 705.5 jit_solution(1602777062990586698)
XLA Ops:
  14.4 42.8 %shard_map.229 = bf16[1024,2048]{1,0:T(8,128)(2,1)} custom-call(bf16[128,2048]{1,0:T(8,128)(2,1)} %fusion.26.own_ref), custom_call_target="tpu_custom_call" | custom-call | tf_op jit(solution)/shard_map/pallas_call | solution.py:362
  59.4 99.9 %shard_map.230 = bf16[4,3104,512]{2,1,0:T(8,128)(2,1)} custom-call(bf16[3104,128]{1,0:T(8,128)(2,1)} %maximum_select_fusion.piece_ref), custom_call_target="tpu_custom_call" | custom-call | tf_op jit(solution)/shard_map/pallas_call | solution.py:362
  162.3 7.3 %slice_bitcast_fusion.2 = (bf16[4,54,8,512]{3,2,1,0:T(8,128)(2,1)S(1)}, bf16[4,54,8,512]{3,2,1,0:T(8,128)(2,1)}, bf16[4,54,8,512]{3,2,1,0:T(8,128)(2,1)}, bf16[4...) fusion(bf16[3104,4,512]{2,0,1:T(8,128)(2,1)} %bitcast.133), kind=kLoop, calls=%fused_computation.21 | loop fusion | bytes 21233664
  175.2 3.6 fusion.122
  196.9 3.5 multiply_convert_fusion.1
  201.4 4.4 convolution_convert_fusion.1.part_ref
  205.8 41.0 %shard_map.231 = f32[128,2048]{1,0:T(8,128)} custom-call(bf16[1024,2048]{1,0:T(8,128)(2,1)} %convolution_convert_fusion.1.part_ref), custom_call_target="tpu_custom_call" | custom-call | tf_op jit(solution)/shard_map/pallas_call | solution.py:362
  249.5 42.1 %shard_map.232 = bf16[1024,2048]{1,0:T(8,128)(2,1)} custom-call(bf16[128,2048]{1,0:T(8,128)(2,1)} %multiply_convert_fusion.3.own_ref), custom_call_target="tpu_custom_call" | custom-call | tf_op jit(solution)/shard_map/pallas_call | solution.py:362
  291.6 5.4 fusion.124
  297.0 8.2 %fusion.5 = (bf16[1024,432]{0,1:T(8,128)(2,1)S(1)}, f32[1024,432]{0,1:T(8,128)S(1)}, f32[432,1024]{1,0:T(8,128)S(1)}) fusion(f32[1024,432]{0,1:T(8,128)} %fusion.124, bf16[432,2048]{1,0:T(8,128)(2,1)} %bitcast.148, bf16[1024,2048]{1,0:T(8,128)(2,1)} %all-gather.2.cloned.1.call-done), kind=kOutput, calls=%fused_computation.30 | convolution fusion | flops 1841135616 | bytes 12156928 | tf_op jit(solution)/shard_map/dot_general | solution.py:471
  311.2 5.7 fusion.125
  320.1 4.4 convolution_convert_fusion.part_ref
  324.6 27.2 %shard_map.233 = f32[128,2048]{1,0:T(8,128)} custom-call(bf16[1024,2048]{1,0:T(8,128)(2,1)} %convolution_convert_fusion.part_ref), custom_call_target="tpu_custom_call" | custom-call | tf_op jit(solution)/shard_map/pallas_call | solution.py:362
  351.7 7.8 %add_convert_fusion.1.part_ref = bf16[1024,2048]{1,0:T(8,128)(2,1)} fusion(f32[1024,2048]{1,0:T(8,128)} %fusion.125, bf16[1024,432]{0,1:T(8,128)(2,1)S(1)} %get-tuple-element.58, bf16[432,2048]{1,0:T(8,128)(2,1)S(1)} %bitcast.147), kind=kOutput, calls=%fused_computation.1 | convolution fusion | flops 1816133632 | bytes 15237120 | tf_op jit(solution)/shard_map/dot_general | solution.py:471
  359.6 30.2 %shard_map.234 = f32[128,2048]{1,0:T(8,128)} custom-call(bf16[1024,2048]{1,0:T(8,128)(2,1)} %add_convert_fusion.1.part_ref), custom_call_target="tpu_custom_call" | custom-call | tf_op jit(solution)/shard_map/pallas_call | solution.py:362
  395.8 41.2 %shard_map.235 = bf16[1024,2048]{1,0:T(8,128)(2,1)} custom-call(bf16[128,2048]{1,0:T(8,128)(2,1)} %fusion.50.own_ref), custom_call_target="tpu_custom_call" | custom-call | tf_op jit(solution)/shard_map/pallas_call | solution.py:362
  437.1 5.6 convolution_convert_fusion.5.refs_4_
  456.3 5.9 fusion.93
  465.4 5.7 fusion.127
  478.6 4.6 fusion.71
  489.3 82.1 %shard_map.237 = f32[3104,128]{1,0:T(8,128)} custom-call(bf16[256,2048]{1,0:T(8,128)(2,1)} %convolution_convert_fusion.9.refs_0_, bf16[256,2048]{1,0:T(8,128)(2,1)} %convolution_convert_fusion.8.refs_1_, bf16[432,2048]{1,0:T(8,128)(2,1)} %convolution_convert_fusion.7.refs_2_, bf16[432,2048]{1,0:T(8,128)(2,1)} %convolution_convert_fusion.6.refs_3_, ...), custom_call_target="tpu_custom_call" | custom-call | tf_op jit(solution)/shard_map/pallas_call | solution.py:362
  577.8 11.7 %add_convert_fusion.part_ref = bf16[1024,2048]{1,0:T(8,128)(2,1)} fusion(f32[1024,2048]{1,0:T(8,128)} %fusion.127, f32[1024,2048]{1,0:T(8,128)} %fusion.93, f32[1024,2048]{1,0:T(8,128)} %fusion.71, bf16[256,2048]{0,1:T(8,128)(2,1)S(1)} %bitcast.139, bf16[1024,128]{0,1:T(8,128)(2,1)} %copy-done.48, bf16[1024,128]{0,1:T(8,128)(2,1)S(1)} %get-tuple-element.91), kind=kOutput, calls=%fused_computation | convolution fusion | flops 1083179008 | bytes 30932992 | tf_op jit(solution)/shard_map/dot_general | solution.py:471
  589.6 28.8 %shard_map.236 = f32[128,2048]{1,0:T(8,128)} custom-call(bf16[1024,2048]{1,0:T(8,128)(2,1)} %add_convert_fusion.part_ref), custom_call_target="tpu_custom_call" | custom-call | tf_op jit(solution)/shard_map/pallas_call | solution.py:362
  620.6 65.8 %all-reduce = (f32[2048]{0:T(1024)}, f32[2048]{0:T(1024)}) all-reduce(f32[2048]{0:T(1024)S(1)} %get-tuple-element.50, f32[2048]{0:T(1024)S(1)} %get-tuple-element.48), channel_id=1, replica_groups=mesh['fsdp'=16,'ctx'=2,'tp'=4] {'fsdp','ctx','tp'}, use_global_device_ids=true, to_apply=%region_13.14 | all-reduce | flops 4096 | bytes 32768 | tf_op jit(solution)/shard_map/psum | solution.py:620
  (281 shorter events, 104.4 us)
Async XLA Ops:
  7.3 289.7 %all-gather.2.cloned.1.call-start = ((), (), s32[]{:S(2)}) async-start(), calls=%async_computation | async-start | bytes 6291456 | tf_op jit(solution)/shard_map/all_gather | solution.py:583
  9.0 48.2 %collective-permute-start = (bf16[3104,64]{0,1:T(8,128)(2,1)S(1)}, bf16[3104,64]{0,1:T(8,128)(2,1)S(1)}, u32[]{:S(2)}, u32[]{:S(2)}) collective-permute-start(bf16[3104,64]{0,1:T(8,128)(2,1)S(1)} %concatenate.65), channel_id=1, source_target_pairs={{0,4},{4,0},{1,5},{5,1},{2,6},{6,2},{3,7},{7,3},{8,12},{12,8},{9,1... | collective-permute-start | bytes 1191944 | tf_op jit(solution)/shard_map/ppermute | solution.py:499
  11.7 45.5 %copy-start.65 = (f32[128]{0:T(128)}, f32[128]{0:T(128)S(1)}, u32[]{:S(2)}) copy-start(f32[128]{0:T(128)S(1)} %fusion.99) | copy-start | bytes 1540
  172.6 6.3 copy-start.12
  183.0 11.3 %copy-start.19 = (bf16[1024,128]{0,1:T(8,128)(2,1)}, bf16[1024,128]{0,1:T(8,128)(2,1)S(1)}, u32[]{:S(2)}) copy-start(bf16[1024,128]{0,1:T(8,128)(2,1)S(1)} %get-tuple-element.95) | copy-start | bytes 786436
  183.0 11.3 %copy-start.21 = (bf16[1024,128]{0,1:T(8,128)(2,1)}, bf16[1024,128]{0,1:T(8,128)(2,1)S(1)}, u32[]{:S(2)}) copy-start(bf16[1024,128]{0,1:T(8,128)(2,1)S(1)} %get-tuple-element.96) | copy-start | bytes 786436
  183.0 11.6 %copy-start.25 = (bf16[512,256]{0,1:T(8,128)(2,1)}, bf16[512,256]{0,1:T(8,128)(2,1)S(1)}, u32[]{:S(2)}) copy-start(bf16[512,256]{0,1:T(8,128)(2,1)S(1)} %fusion.84) | copy-start | bytes 786436
  183.1 11.9 %copy-start.27 = (bf16[512,256]{0,1:T(8,128)(2,1)}, bf16[512,256]{0,1:T(8,128)(2,1)S(1)}, u32[]{:S(2)}) copy-start(bf16[512,256]{0,1:T(8,128)(2,1)S(1)} %pad_maximum_fusion.12) | copy-start | bytes 786436
  183.8 12.3 %copy-start.33 = (bf16[512,512]{1,0:T(8,128)(2,1)}, bf16[512,512]{1,0:T(8,128)(2,1)S(1)}, u32[]{:S(2)}) copy-start(bf16[512,512]{1,0:T(8,128)(2,1)S(1)} %fusion.18) | copy-start | bytes 1572868
  184.3 11.2 %copy-start.35 = (bf16[512,512]{1,0:T(8,128)(2,1)}, bf16[512,512]{1,0:T(8,128)(2,1)S(1)}, u32[]{:S(2)}) copy-start(bf16[512,512]{1,0:T(8,128)(2,1)S(1)} %fusion.17) | copy-start | bytes 1572868
  190.1 10.4 %copy-start.42 = (bf16[4,54,8,512]{3,2,0,1:T(8,128)(2,1)}, bf16[4,54,8,512]{3,2,0,1:T(8,128)(2,1)S(1)}, u32[]{:S(2)}) copy-start(bf16[4,54,8,512]{3,2,0,1:T(8,128)(2,1)S(1)} %copy.149) | copy-start | bytes 5308420
  249.5 42.1 %copy-start.44 = (bf16[4,54,8,512]{3,2,0,1:T(8,128)(2,1)S(1)}, bf16[4,54,8,512]{3,2,0,1:T(8,128)(2,1)}, u32[]{:S(2)}) copy-start(bf16[4,54,8,512]{3,2,0,1:T(8,128)(2,1)} %copy.150) | copy-start | bytes 5308420
  297.0 8.3 %copy-start.16 = (bf16[1024,2048]{1,0:T(8,128)(2,1)S(1)}, bf16[1024,2048]{1,0:T(8,128)(2,1)}, u32[]{:S(2)}) copy-start(bf16[1024,2048]{1,0:T(8,128)(2,1)} %shard_map.232) | copy-start | bytes 12582916
  297.0 8.3 %copy-start.46 = (bf16[4,54,8,512]{3,2,0,1:T(8,128)(2,1)S(1)}, bf16[4,54,8,512]{3,2,0,1:T(8,128)(2,1)}, u32[]{:S(2)}) copy-start(bf16[4,54,8,512]{3,2,0,1:T(8,128)(2,1)} %copy.151) | copy-start | bytes 5308420
  297.0 8.3 %copy-start.70 = (f32[1024,432]{0,1:T(8,128)S(1)}, f32[1024,432]{0,1:T(8,128)}, u32[]{:S(2)}) copy-start(f32[1024,432]{0,1:T(8,128)} %fusion.124) | copy-start | bytes 5308420
  308.0 12.1 %copy-start.71 = (bf16[1024,432]{0,1:T(8,128)(2,1)}, bf16[1024,432]{0,1:T(8,128)(2,1)S(1)}, u32[]{:S(2)}) copy-start(bf16[1024,432]{0,1:T(8,128)(2,1)S(1)} %get-tuple-element.72) | copy-start | bytes 2654212
  395.8 41.2 %copy-start.74 = (bf16[1024,432]{0,1:T(8,128)(2,1)S(1)}, bf16[1024,432]{0,1:T(8,128)(2,1)}, u32[]{:S(2)}) copy-start(bf16[1024,432]{0,1:T(8,128)(2,1)} %copy-done.73) | copy-start | bytes 2654212
  476.3 6.9 copy-start.48
  575.1 113.8 %collective-permute-start.1 = (f32[3104,64]{0,1:T(8,128)}, f32[3104,64]{0,1:T(8,128)}, u32[]{:S(2)}, u32[]{:S(2)}) collective-permute-start(f32[3104,64]{0,1:T(8,128)} %copy.121), channel_id=1, source_target_pairs={{0,4},{4,0},{1,5},{5,1},{2,6},{6,2},{3,7},{7,3},{8,12},{12,8},{9,1... | collective-permute-start | bytes 2383880 | tf_op jit(solution)/shard_map/ppermute | solution.py:499
  589.5 28.8 %copy-start.59 = (f32[2048]{0:T(1024)S(1)}, f32[2048]{0:T(1024)}, u32[]{:S(2)}) copy-start(f32[2048]{0:T(1024)} %param.17) | copy-start | bytes 24580
  589.5 28.8 %copy-start.64 = (f32[128]{0:T(128)S(1)}, f32[128]{0:T(128)}, u32[]{:S(2)}) copy-start(f32[128]{0:T(128)} %copy-done.63) | copy-start | bytes 1540
  589.5 30.5 %copy-start.68 = (f32[128]{0:T(128)S(1)}, f32[128]{0:T(128)}, u32[]{:S(2)}) copy-start(f32[128]{0:T(128)} %copy-done.67) | copy-start | bytes 1540
  589.5 30.5 %copy-start.66 = (f32[128]{0:T(128)S(1)}, f32[128]{0:T(128)}, u32[]{:S(2)}) copy-start(f32[128]{0:T(128)} %copy-done.65) | copy-start | bytes 1540
  618.3 68.0 %copy-start.5 = (f32[128,2048]{1,0:T(8,128)S(1)}, f32[128,2048]{1,0:T(8,128)}, u32[]{:S(2)}) copy-start(f32[128,2048]{1,0:T(8,128)} %copy-done.4) | copy-start | bytes 3145732
  (54 other events, 114.4 us)
Sparse Core Ops, SparseCore 0:
  9.7 20.0 all-gather.1

commit v2 on v1

--- a/solution.py
+++ b/solution.py
@@ -372,22 +372,6 @@
     )(*[array for array, _ in ins])
 
 
-def weights_in(piece, cid):
-    def kernel(piece_ref, out_ref, send, recv, local):
-        net = Net(send, recv)
-        own = pltpu.make_async_copy(piece_ref, out_ref.at[net.x, :, lanes(net.z)], local.at[0])
-        own.start()
-        net.greet(XZ_HOPS)
-        own.wait()
-        for stage in gather_weights(net, out_ref, 0, ROWS):
-            stage()
-
-    (out,) = call(
-        kernel, [(jax.ShapeDtypeStruct((4, ROWS, 512), BF), False)], [(piece, False)], [], 16, cid
-    )
-    return out
-
-
 def grads_out(parts, cid):
     def kernel(*refs):
         parts_refs, out_ref, total = refs[:8], refs[8], refs[9]
@@ -427,17 +411,22 @@
 
 
 def rows_in(own, cid):
-    def kernel(own_ref, out_ref, send, recv, local):
+    def kernel(own_ref, out_ref, rows, send, recv, local):
         net = Net(send, recv)
         at = pl.ds(pl.multiple_of(net.c * 512 + net.t * 128, 128), 128)
-        load = pltpu.make_async_copy(own_ref, out_ref.at[at, :], local.at[0])
+        load = pltpu.make_async_copy(own_ref, rows.at[at, :], local.at[0])
         load.start()
         net.greet(Y_HOPS)
         load.wait()
-        for stage in gather_rows(net, out_ref):
+        for stage in gather_rows(net, rows):
             stage()
-
-    (out,) = call(kernel, [(jax.ShapeDtypeStruct((SEQ, D), BF), False)], [(own, False)], [], 9, cid)
+        store = pltpu.make_async_copy(rows, out_ref, local.at[0])
+        store.start()
+        store.wait()
+
+    (out,) = call(
+        kernel, [(jax.ShapeDtypeStruct((SEQ, D), BF), False)], [(own, False)], [pltpu.VMEM((SEQ, D), BF)], 9, cid
+    )
     return out
 
 
@@ -476,18 +465,211 @@
 TN = ((0,), (0,))
 
 
+def normal(rows, width):
+    centred = rows - jnp.sum(rows, axis=-1, keepdims=True) * (1.0 / width)
+    spread = jnp.sum(centred * centred, axis=-1, keepdims=True) * (1.0 / width)
+    return centred, lax.rsqrt(spread + EPSILON)
+
+
+def loop(count, step, body):
+    def turn(i, carry):
+        body(pl.ds(pl.multiple_of(i * step, step), step))
+        return carry
+
+    lax.fori_loop(0, count // step, turn, 0)
+
+
+def times(rows_ref, rows, weights, k):
+    total = None
+    for x in range(4):
+        part = dot(rows_ref[rows, x * 512 : x * 512 + 512], weights[x, STARTS[k] : STARTS[k] + SIZES[k], :], NT)
+        total = part if total is None else total + part
+    return total
+
+
+def forward(piece, inputs, carried_state, attn_gain, mlp_gain, cosine, sine, row_mask, lam, cid):
+    def kernel(
+        piece_ref, in_ref, carried_ref, gain_one, gain_two, cos_ref, sin_ref, mask_ref, lam_ref,
+        weights_out, one_out, two_out, q_ref, k_ref, v_ref, s_ref, mix_ref, norm_ref, dev_ref, mixed_ref, prior_ref,
+        hidden_ref,
+        weights, one, two, carried, part, *rest,
+    ):
+        bufs, (send, recv, local) = rest[:5], rest[5:]
+        net = Net(send, recv)
+        c, t = net.c, net.t
+        load = pltpu.make_async_copy(piece_ref, weights.at[net.x, :, lanes(net.z)], local.at[0])
+        load.start()
+        load_state = pltpu.make_async_copy(carried_ref.at[0, c], carried, local.at[1])
+        load_state.start()
+        own = c * 512 + t * 128
+
+        def norm_rows(source, gain, rows_ref):
+            def body(at):
+                centred, dev = normal(source[at, :].astype(F32), D)
+                to = pl.ds(pl.multiple_of(own + at.start, 16), at.size)
+                rows_ref[to, :] = (centred * dev * gain[...]).astype(BF)
+
+            loop(128, 32, body)
+
+        norm_rows(in_ref, gain_one, one)
+        net.greet(XZ_HOPS + Y_HOPS)
+        y1 = gather_rows(net, one)
+        g1, g2, g3, g4 = (
+            gather_weights(net, weights, lo, hi) for lo, hi in ((0, 1376), (1376, 1808), (1808, 2672), (2672, 3104))
+        )
+        load.wait()
+        g1[0]()
+        y1[0]()
+        g1[1]()
+        g1[2]()
+        y1[1]()
+        g2[0]()
+        y1[2]()
+        g2[1]()
+        g1[3]()
+        g2[2]()
+        g1[4]()
+
+        def project(at):
+            cs, sn = cos_ref[at, :], sin_ref[at, :]
+            for k, ref in ((0, q_ref), (1, k_ref)):
+                raw = times(one, at, weights, k)
+                former, latter = raw[:, :128], raw[:, 128:]
+                ref[at, :128] = (former * cs - latter * sn).astype(BF)
+                ref[at, 128:] = (former * sn + latter * cs).astype(BF)
+            v_ref[at, :] = (times(one, at, weights, 2) * mask_ref[at, :]).astype(BF)
+            s_ref[at, :] = times(one, at, weights, 3)
+
+        loop(SEQ, 256, project)
+        g2[3]()
+        g3[0]()
+
+        decay = lam_ref[0:1, 0:1]
+        load_state.wait()
+        prior_ref[0] = carried[...].astype(BF)
+        far = lax.broadcasted_iota(jnp.int32, (HALF, 1), 0).astype(F32)
+        tail = jnp.exp((HALF - 1.0 - far) * decay)
+        local_state = dot((k_ref[:HALF, :].astype(F32) * tail).astype(BF), v_ref[:HALF, :], TN)
+        prior_ref[1] = (jnp.exp(HALF * decay) * carried[...] + local_state).astype(BF)
+
+        for stretch in range(2):
+            keys = pl.ds(stretch * HALF, HALF)
+
+            def retain(rows, stretch=stretch, keys=keys):
+                at = pl.ds(pl.multiple_of(stretch * HALF + rows.start, rows.size), rows.size)
+                n = lax.broadcasted_iota(jnp.int32, (rows.size, HALF), 0) + rows.start
+                distance = (n - lax.broadcasted_iota(jnp.int32, (rows.size, HALF), 1)).astype(F32)
+                fade = jnp.where(distance >= 0.0, jnp.exp(jnp.maximum(distance, 0.0) * decay), 0.0)
+                mixing = (dot(q_ref[at, :], k_ref[keys, :], NT) * fade).astype(BF)
+                mix_ref[at, :] = mixing
+                ahead = lax.broadcasted_iota(jnp.int32, (rows.size, 1), 0) + rows.start + 1
+                head = jnp.exp(ahead.astype(F32) * decay)
+                retained = dot(mixing, v_ref[keys, :], NN) + dot(q_ref[at, :], prior_ref[stretch], NN) * head
+                centred, dev = normal(retained, VDIM)
+                normed = centred * dev
+                norm_ref[at, :] = normed
+                dev_ref[at, :] = dev
+                swish = s_ref[at, :]
+                mixed_ref[at, :] = (mask_ref[at, :] * (swish * jax.nn.sigmoid(swish)) * normed).astype(BF)
+
+            loop(HALF, 128, retain)
+
+        g2[4]()
+        g3[1]()
+
+        def out_rows(base):
+            def body(rows):
+                at = pl.ds(pl.multiple_of(base + rows.start, rows.size), rows.size)
+                for x in range(4):
+                    got = dot(mixed_ref[at, :], weights[x, STARTS[4] : STARTS[4] + VDIM, :], NN)
+                    part[at, x * 512 : x * 512 + 512] = got.astype(BF)
+
+            loop(HALF, 256, body)
+
+        def take(at, value):
+            hidden_ref[at, :] = in_ref[at, :].astype(F32) + value
+
+        r1 = scatter_rows(net, part, bufs, take)
+        out_rows((1 - c) * HALF)
+        r1[0]()
+        out_rows(c * HALF)
+        g3[2]()
+        r1[1]()
+        g4[0]()
+        r1[2]()
+        g3[3]()
+        g4[1]()
+        r1[3]()
+        norm_rows(hidden_ref, gain_two, two)
+        y2 = gather_rows(net, two)
+        y2[0]()
+        g3[4]()
+        g4[2]()
+        store_one = pltpu.make_async_copy(one, one_out, local.at[2])
+        store_one.start()
+        y2[1]()
+        g4[3]()
+        y2[2]()
+        store_two = pltpu.make_async_copy(two, two_out, local.at[3])
+        store_two.start()
+        g4[4]()
+        stores = [store_one, store_two]
+        for x in range(4):
+            store = pltpu.make_async_copy(weights.at[x], weights_out.at[:, pl.ds(x * 512, 512)], local.at[4 + x])
+            store.start()
+            stores.append(store)
+        for store in stores:
+            store.wait()
+
+    def shape(*dims, kind=BF):
+        return jax.ShapeDtypeStruct(dims, kind)
+
+    return call(
+        kernel,
+        [
+            (shape(ROWS, D), False),
+            (shape(SEQ, D), False),
+            (shape(SEQ, D), False),
+            (shape(SEQ, KDIM), True),
+            (shape(SEQ, KDIM), True),
+            (shape(SEQ, VDIM), True),
+            (shape(SEQ, VDIM, kind=F32), True),
+            (shape(SEQ, HALF), True),
+            (shape(SEQ, VDIM, kind=F32), True),
+            (shape(SEQ, 1, kind=F32), True),
+            (shape(SEQ, VDIM), True),
+            (shape(2, KDIM, VDIM), True),
+            (shape(128, D, kind=F32), True),
+        ],
+        [
+            (piece, False),
+            (inputs, True),
+            (carried_state, False),
+            (attn_gain, True),
+            (mlp_gain, True),
+            (cosine, True),
+            (sine, True),
+            (row_mask, True),
+            (lam, True),
+        ],
+        [
+            pltpu.VMEM((4, ROWS, 512), BF),
+            pltpu.VMEM((SEQ, D), BF),
+            pltpu.VMEM((SEQ, D), BF),
+            pltpu.VMEM((KDIM, VDIM), F32),
+            pltpu.VMEM((SEQ, D), BF),
+        ]
+        + ROW_BUFS,
+        100,
+        cid,
+    )
+
+
 def layer_norm(rows_in, gain):
     centre = jnp.mean(rows_in, axis=-1, keepdims=True)
     centred = rows_in - centre
     spread = jnp.mean(centred * centred, axis=-1, keepdims=True)
     return centred * lax.rsqrt(spread + EPSILON) * gain
-
-
-def group_norm(values_in):
-    centre = jnp.mean(values_in, axis=-1, keepdims=True)
-    centred = values_in - centre
-    spread = jnp.mean(centred * centred, axis=-1, keepdims=True)
-    return centred * lax.rsqrt(spread + EPSILON)
 
 
 def rotate(field, cosine, sine):
@@ -532,46 +714,29 @@
 
     mine, got = for_core(core), swap_cores(for_core(1 - core))
     piece = jnp.where(core == 0, jnp.concatenate([mine, got], axis=1), jnp.concatenate([got, mine], axis=1))
-    weights = weights_in(piece, 1)
-    weights = weights.transpose(1, 0, 2).reshape(ROWS, D)
-    w_query, w_key, w_value, w_swish, w_out, w_gate, w_up, w_down = (
-        weights[s : s + n] for s, n in zip(STARTS, SIZES)
-    )
     position = jnp.arange(SEQ, dtype=jnp.int32)
     row_mask = (position < seq_lengths[0]).astype(F32)[:, None]
     frequency = jnp.power(10000.0, -jnp.arange(128).astype(F32) / 128)
     angles = position.astype(F32)[:, None] * frequency[None, :]
     cosine, sine = jnp.cos(angles), jnp.sin(angles)
     decay = -jnp.power(2.0, 5.0 - head.astype(F32)) / SEQ
+    (
+        weights, rows_one, rows_two, queries, keys_rot, values_kept, swish_raw, mix, normed, dev, mixed, prior, hidden
+    ) = forward(
+        piece, inputs, carried_state, attn_gain[None, :], mlp_gain[None, :], cosine, sine, row_mask,
+        jnp.full((8, 128), decay, F32), 1
+    )
+    w_query, w_key, w_value, w_swish, w_out, w_gate, w_up, w_down = (
+        weights[s : s + n] for s, n in zip(STARTS, SIZES)
+    )
     local_pos = jnp.arange(HALF).astype(F32)
     tail_fac = jnp.exp((HALF - 1.0 - local_pos) * decay)[:, None]
     head_fac = jnp.exp((local_pos + 1.0) * decay)[:, None]
-    span = jnp.exp(HALF * decay)
     distance = local_pos[:, None] - local_pos[None, :]
     decay_mask = jnp.where(distance >= 0.0, jnp.exp(jnp.maximum(distance, 0.0) * decay), 0.0)
-    carried = lax.dynamic_index_in_dim(carried_state[0], core, 0, keepdims=False)
-
     inputs_wide = inputs.astype(F32)
-    rows_one = rows_in(layer_norm(inputs_wide, attn_gain).astype(BF), 2)
-    queries = rotate(dot(rows_one, w_query, NT), cosine, sine).astype(BF)
-    keys_rot = rotate(dot(rows_one, w_key, NT), cosine, sine).astype(BF)
-    values_kept = (dot(rows_one, w_value, NT) * row_mask).astype(BF)
-    swish_raw = dot(rows_one, w_swish, NT)
     stretch = lambda a: (a[:HALF], a[HALF:])
-    qs, ks, vs = stretch(queries), stretch(keys_rot), stretch(values_kept)
-    mixing = [(dot(q, k, NT) * decay_mask).astype(BF) for q, k in zip(qs, ks)]
-    local_state = dot((ks[0] * tail_fac).astype(BF), vs[0], TN)
-    prior = [carried.astype(BF), (span * carried + local_state).astype(BF)]
-    retained = jnp.concatenate(
-        [dot(m, v, NN) + dot(q, p, NN) * head_fac for m, v, q, p in zip(mixing, vs, qs, prior)], axis=0
-    )
-
-    def gate_piece(swish_in, retained_in):
-        return row_mask * jax.nn.silu(swish_in) * group_norm(retained_in)
-
-    mixed = gate_piece(swish_raw, retained).astype(BF)
-    hidden = inputs_wide + rows_out(dot(mixed, w_out, NN).astype(BF), 3)
-    rows_two = rows_in(layer_norm(hidden, mlp_gain).astype(BF), 4)
+    qs, ks, vs, mixing = stretch(queries), stretch(keys_rot), stretch(values_kept), stretch(mix)
     gate_pre = dot(rows_two, w_gate, NT)
     up_pre = dot(rows_two, w_up, NT)
 
@@ -595,8 +760,13 @@
     mid_rows = rows_in(grad_hidden.astype(BF), 7)
     out_part = dot(mixed, mid_rows, TN)
     grad_mixed = dot(mid_rows, w_out, NT)
-    _, gate_pull = jax.vjp(gate_piece, swish_raw, retained)
-    grad_swish, grad_retained = (g.astype(BF) for g in gate_pull(grad_mixed))
+    sig = jax.nn.sigmoid(swish_raw)
+    grad_swish = (row_mask * grad_mixed * normed * (sig * (1.0 + swish_raw * (1.0 - sig)))).astype(BF)
+    grad_normed = row_mask * grad_mixed * (swish_raw * sig)
+    grad_normed = grad_normed - jnp.mean(grad_normed, axis=-1, keepdims=True) - normed * jnp.mean(
+        grad_normed * normed, axis=-1, keepdims=True
+    )
+    grad_retained = (grad_normed * dev).astype(BF)
     rs = stretch(grad_retained)
     grad_local = dot((qs[1] * head_fac).astype(BF), rs[1], TN).astype(BF)
     gq, gk, gv = [], [], []

time: 707 us -> 579 us (0.82); the launches traced: 705 us -> 570 us
  Pallas kernels: 435 us -> 330 us
  local copies, waits for them, and re-layouts: 43.2 us -> 17.3 us
    pallas_call x9 -> x6, Pallas kernels: 435 us -> 330 us  [call(): pl.pallas_call(kernel, out_shape=[shape for shape, _ in outs], in_specs=[...]
    unnamed x174 -> x86, local copies, waits for them, and re-layouts: 26.4 us -> 10.9 us
    slice x9 -> x0, local copies, waits for them, and re-layouts: 12.3 us -> none  [on_device(): weights[s:s + n]]
    dot_general x44 -> x32, matrix products: 114 us -> 109 us  [dot(): return lax.dot_general(a, b, (dims, ((), ())), preferred_element_type=F32)]
  transfers between devices with their start and end apart: 3 -> 3, of which waited for: 0 -> 0; matrix products, arithmetic and copies ran while one was open for 10% -> 6% of each run, Pallas kernels for 36% -> 26%
where the time goes in v2:
time: 579 us; the launch traced here: 570 us
  Pallas kernels  330 us (57%)
  matrix products  109 us (19%)
  blocking collectives  65.8 us (11%)
  other arithmetic  28.2 us (5%)
  local copies, waits for them, and re-layouts  17.3 us (3%)
  between operations  16 us (3%)
    pallas_call x6, Pallas kernels, call(): pl.pallas_call(kernel, out_shape=[shape for shape, _ in outs], in_specs=[...  330 us
    dot_general x32, matrix products, dot(): return lax.dot_general(a, b, (dims, ((), ())), preferred_element_type=F32)  109 us
    psum x1, blocking collectives, on_device(): lax.psum((attn_gain_part, mlp_gain_part), ('fsdp', 'ctx', 'tp'))  65.8 us
  transfers between devices with their start and end apart: 3, of which 0 were waited for; matrix products, arithmetic and copies ran while one was open for 6% of the time, Pallas kernels for 26%

profile of v2, /device:TPU:1, one launch (start us, length us, event | category | flops | bytes accessed | tf_op | source)
XLA Modules:
  0.0 570.4 jit_solution(15640431767869730869)
XLA Ops:
  21.3 122.6 %shard_map.229 = (bf16[3104,2048]{1,0:T(8,128)(2,1)}, bf16[1024,2048]{1,0:T(8,128)(2,1)}, bf16[1024,2048]{1,0:T(8,128)(2,1)}, bf16[1024,256]{1,0:T(8,128)(2,1)},...) custom-call(bf16[3104,128]{1,0:T(8,128)(2,1)} %maximum_select_fusion, ...), custom_call_target="tpu_custom_call" | custom-call | tf_op jit(solution)/shard_map/pallas_call | solution.py:362
  146.9 6.4 %fusion.22 = f32[1024,432]{1,0:T(8,128)} fusion(bf16[1024,2048]{1,0:T(8,128)(2,1)} %get-tuple-element.26, bf16[3104,2048]{1,0:T(8,128)(2,1)} %get-tuple-element.27), kind=kOutput, calls=%fused_computation.55 | convolution fusion | flops 1811939328 | bytes 7733248 | tf_op jit(solution)/shard_map/dot_general | solution.py:460
  153.3 9.5 %fusion.2 = (bf16[1024,432]{1,0:T(8,128)(2,1)S(1)}, f32[1024,432]{1,0:T(8,128)S(1)}, f32[432,1024]{0,1:T(8,128)S(1)}) fusion(f32[1024,432]{1,0:T(8,128)} %fusion.22, bf16[1024,2048]{1,0:T(8,128)(2,1)} %all-gather.2.cloned.1.call-done, bf16[3104,2048]{1,0:T(8,128)(2,1)} %get-tuple-element.27), kind=kOutput, calls=%fused_computation.17 | convolution fusion | flops 1841135616 | bytes 12484608 | tf_op jit(solution)/shard_map/dot_general | solution.py:460
  162.8 4.6 add_convert_fusion.2
  167.5 3.3 convolution_convert_fusion.3.refs_5_
  170.7 7.1 %fusion.20 = f32[1024,2048]{1,0:T(8,128)} fusion(bf16[1024,432]{1,0:T(8,128)(2,1)S(1)} %get-tuple-element.102, bf16[3104,2048]{1,0:T(8,128)(2,1)} %get-tuple-element.27), kind=kOutput, calls=%fused_computation.53 | convolution fusion | flops 1811939328 | bytes 11042816 | tf_op jit(solution)/shard_map/dot_general | solution.py:460
  177.9 3.4 convolution_convert_fusion.2.refs_6_
  181.2 5.9 %convolution_convert_fusion.part_ref = bf16[1024,2048]{1,0:T(8,128)(2,1)} fusion(bf16[1024,432]{1,0:T(8,128)(2,1)S(1)} %get-tuple-element.103, bf16[3104,2048]{1,0:T(8,128)(2,1)} %get-tuple-element.27), kind=kOutput, calls=%fused_computation.2 | convolution fusion | flops 1814036480 | bytes 6848512 | tf_op jit(solution)/shard_map/dot_general | solution.py:460
  187.1 29.1 %shard_map.230 = f32[128,2048]{1,0:T(8,128)} custom-call(bf16[1024,2048]{1,0:T(8,128)(2,1)} %convolution_convert_fusion.part_ref), custom_call_target="tpu_custom_call" | custom-call | tf_op jit(solution)/shard_map/pallas_call | solution.py:362
  216.2 8.4 %add_convert_fusion.1.part_ref = bf16[1024,2048]{1,0:T(8,128)(2,1)} fusion(f32[1024,2048]{1,0:T(8,128)} %fusion.20, bf16[1024,432]{1,0:T(8,128)(2,1)S(1)} %get-tuple-element.99, bf16[3104,2048]{1,0:T(8,128)(2,1)} %get-tuple-element.27), kind=kOutput, calls=%fused_computation.1 | convolution fusion | flops 1816133632 | bytes 15237120 | tf_op jit(solution)/shard_map/dot_general | solution.py:460
  224.6 40.8 %shard_map.231 = f32[128,2048]{1,0:T(8,128)} custom-call(bf16[1024,2048]{1,0:T(8,128)(2,1)} %add_convert_fusion.1.part_ref), custom_call_target="tpu_custom_call" | custom-call | tf_op jit(solution)/shard_map/pallas_call | solution.py:362
  270.5 27.1 %shard_map.232 = bf16[1024,2048]{1,0:T(8,128)(2,1)} custom-call(bf16[128,2048]{1,0:T(8,128)(2,1)} %fusion.47.own_ref), custom_call_target="tpu_custom_call" | custom-call | tf_op jit(solution)/shard_map/pallas_call | solution.py:362
  297.6 5.2 fusion.12
  310.9 7.3 %fusion.10 = f32[1024,2048]{1,0:T(8,128)} fusion(bf16[3104,2048]{1,0:T(8,128)(2,1)} %get-tuple-element.27, f32[512,432]{1,0:T(8,128)S(1)} %fusion.58, f32[512,432]{1,0:T(8,128)S(1)} %convolution_add_fusion, f32[1024]{0:T(1024)S(1)} %fusion.87), kind=kOutput, calls=%fused_computation.41 | convolution fusion | flops 1813266432 | bytes 11931648 | tf_op jit(solution)/shard_map/dot_general | solution.py:460
  318.2 3.4 convolution_convert_fusion.6.refs_2_
  321.6 3.3 convolution_convert_fusion.5.refs_3_
  324.9 7.2 %fusion.8 = f32[1024,2048]{1,0:T(8,128)} fusion(bf16[1024,432]{1,0:T(8,128)(2,1)S(1)} %get-tuple-element.101, bf16[3104,2048]{1,0:T(8,128)(2,1)} %get-tuple-element.27), kind=kOutput, calls=%fused_computation.39 | convolution fusion | flops 1811939328 | bytes 11042816 | tf_op jit(solution)/shard_map/dot_general | solution.py:460
  338.4 6.0 %fusion.41 = f32[1024,2048]{1,0:T(8,128)} fusion(bf16[3104,2048]{1,0:T(8,128)(2,1)} %get-tuple-element.27, bf16[1024,128]{1,0:T(8,128)(2,1)S(1)} %get-tuple-element.143, bf16[1024,128]{1,0:T(8,128)(2,1)S(1)} %get-tuple-element.144), kind=kOutput, calls=%fused_computation.94 | convolution fusion | flops 1074790400 | bytes 9961472 | tf_op jit(solution)/shard_map/dot_general | solution.py:460
  344.4 3.3 convolution_convert_fusion.4.refs_4_
  353.2 82.6 %shard_map.234 = f32[3104,128]{1,0:T(8,128)} custom-call(bf16[256,2048]{1,0:T(8,128)(2,1)} %convolution_convert_fusion.8.refs_0_, bf16[256,2048]{1,0:T(8,128)(2,1)} %convolution_convert_fusion.7.refs_1_, bf16[432,2048]{1,0:T(8,128)(2,1)} %convolution_convert_fusion.6.refs_2_, bf16[432,2048]{1,0:T(8,128)(2,1)} %convolution_convert_fusion.5.refs_3_, ...), custom_call_target="tpu_custom_call" | custom-call | tf_op jit(solution)/shard_map/pallas_call | solution.py:362
  435.8 3.6 slice_select_fusion
  443.9 11.4 %add_convert_fusion.part_ref = bf16[1024,2048]{1,0:T(8,128)(2,1)} fusion(f32[1024,2048]{1,0:T(8,128)} %fusion.8, f32[1024,2048]{1,0:T(8,128)} %fusion.10, f32[1024,2048]{1,0:T(8,128)} %fusion.41, bf16[3104,2048]{1,0:T(8,128)(2,1)} %get-tuple-element.27, bf16[1024,128]{1,0:T(8,128)(2,1)S(1)} %get-tuple-element.123, bf16[1024,128]{1,0:T(8,128)(2,1)S(1)} %get-tuple-element.122), kind=kOutput, calls=%fused_computation | convolution fusion | flops 1083179008 | bytes 30932992 | tf_op jit(solution)/shard_map/dot_general | solution.py:460
  455.3 27.6 %shard_map.233 = f32[128,2048]{1,0:T(8,128)} custom-call(bf16[1024,2048]{1,0:T(8,128)(2,1)} %add_convert_fusion.part_ref), custom_call_target="tpu_custom_call" | custom-call | tf_op jit(solution)/shard_map/pallas_call | solution.py:362
  485.2 65.8 %all-reduce = (f32[2048]{0:T(1024)}, f32[2048]{0:T(1024)}) all-reduce(f32[2048]{0:T(1024)S(1)} %get-tuple-element.90, f32[2048]{0:T(1024)S(1)} %get-tuple-element.86), channel_id=1, replica_groups=mesh['fsdp'=16,'ctx'=2,'tp'=4] {'fsdp','ctx','tp'}, use_global_device_ids=true, to_apply=%region_11.12 | all-reduce | flops 4096 | bytes 32768 | tf_op jit(solution)/shard_map/psum | solution.py:790
  (162 shorter events, 59.5 us)
Async XLA Ops:
  7.2 1.5 copy-start.24
  7.3 1.5 copy-start.25
  7.3 146.1 %all-gather.2.cloned.1.call-start = ((), (), s32[]{:S(2)}) async-start(), calls=%async_computation | async-start | bytes 6291456 | tf_op jit(solution)/shard_map/all_gather | solution.py:748
  8.7 4.5 copy-start.3
  8.8 4.6 copy-start.11
  9.8 8.8 %collective-permute-start = (bf16[3104,64]{0,1:T(8,128)(2,1)}, bf16[3104,64]{0,1:T(8,128)(2,1)S(1)}, u32[]{:S(2)}, u32[]{:S(2)}) collective-permute-start(bf16[3104,64]{0,1:T(8,128)(2,1)} %concatenate.54), channel_id=1, source_target_pairs={{0,4},{4,0},{1,5},{5,1},{2,6},{6,2},{3,7},{7,3},{8,12},{12,8},{9,1... | collective-permute-start | bytes 1191944 | tf_op jit(solution)/shard_map/ppermute | solution.py:681
  143.9 2.7 copy-start.2
  153.3 9.5 %copy-start.28 = (bf16[1024,2048]{1,0:T(8,128)(2,1)S(1)}, bf16[1024,2048]{1,0:T(8,128)(2,1)}, u32[]{:S(2)}) copy-start(bf16[1024,2048]{1,0:T(8,128)(2,1)} %get-tuple-element.26) | copy-start | bytes 12582916
  153.3 9.5 %copy-start.30 = (f32[1024,432]{1,0:T(8,128)S(1)}, f32[1024,432]{1,0:T(8,128)}, u32[]{:S(2)}) copy-start(f32[1024,432]{1,0:T(8,128)} %fusion.22) | copy-start | bytes 5308420
  224.6 40.8 %copy-start.23 = (f32[2048]{0:T(1024)S(1)}, f32[2048]{0:T(1024)}, u32[]{:S(2)}) copy-start(f32[2048]{0:T(1024)} %param.23) | copy-start | bytes 24580
  265.4 1.8 copy-start.5
  265.4 1.8 copy-start.8
  297.6 5.3 copy-start.6
  297.6 5.3 copy-start.9
  310.9 7.3 %copy-start.27 = (bf16[1024,2048]{1,0:T(8,128)(2,1)S(1)}, bf16[1024,2048]{1,0:T(8,128)(2,1)}, u32[]{:S(2)}) copy-start(bf16[1024,2048]{1,0:T(8,128)(2,1)} %get-tuple-element.36) | copy-start | bytes 12582916
  324.9 7.5 %copy-start.13 = (bf16[2,256,432]{2,1,0:T(8,128)(2,1)S(1)}, bf16[2,256,432]{2,1,0:T(8,128)(2,1)}, u32[]{:S(2)}) copy-start(bf16[2,256,432]{2,1,0:T(8,128)(2,1)} %get-tuple-element.33) | copy-start | bytes 1327108
  338.4 6.0 %copy-start.7 = (bf16[1024,2048]{1,0:T(8,128)(2,1)S(1)}, bf16[1024,2048]{1,0:T(8,128)(2,1)}, u32[]{:S(2)}) copy-start(bf16[1024,2048]{1,0:T(8,128)(2,1)} %shard_map.232) | copy-start | bytes 12582916
  338.4 6.0 %copy-start.29 = (bf16[1024,432]{1,0:T(8,128)(2,1)S(1)}, bf16[1024,432]{1,0:T(8,128)(2,1)}, u32[]{:S(2)}) copy-start(bf16[1024,432]{1,0:T(8,128)(2,1)} %get-tuple-element.37) | copy-start | bytes 2654212
  347.7 2.3 copy-start.26
  441.3 112.2 %collective-permute-start.1 = (f32[3104,64]{0,1:T(8,128)S(1)}, f32[3104,64]{0,1:T(8,128)}, u32[]{:S(2)}, u32[]{:S(2)}) collective-permute-start(f32[3104,64]{0,1:T(8,128)S(1)} %copy.146), channel_id=1, source_target_pairs={{0,4},{4,0},{1,5},{5,1},{2,6},{6,2},{3,7},{7,3},{8,12},{12,8},{9,1... | collective-permute-start | bytes 2383880 | tf_op jit(solution)/shard_map/ppermute | solution.py:681
  455.3 27.7 %copy-start.4 = (bf16[128,2048]{1,0:T(8,128)(2,1)S(1)}, bf16[128,2048]{1,0:T(8,128)(2,1)}, u32[]{:S(2)}) copy-start(bf16[128,2048]{1,0:T(8,128)(2,1)} %in_ref.1) | copy-start | bytes 1572868
  455.3 27.7 %copy-start.22 = (f32[2048]{0:T(1024)S(1)}, f32[2048]{0:T(1024)}, u32[]{:S(2)}) copy-start(f32[2048]{0:T(1024)} %param.17) | copy-start | bytes 24580
  483.0 1.7 copy-start.1
  553.5 1.8 copy-start
  (10 other events, 11.3 us)
Sparse Core Ops, SparseCore 0:
  9.7 20.7 all-gather.1

commit v3 on v2

--- a/solution.py
+++ b/solution.py
@@ -299,10 +299,11 @@
 ]
 
 
-def scatter_rows(net, ref, bufs, out):
+def scatter_rows(net, ref, bufs, out, source=None):
     c, t = net.c, net.t
     other, far_a, far_b, near_a, near_b = bufs
-    side = net.copy(ref.at[pl.ds(pl.multiple_of((1 - c) * 512, 512), 512), :], other, dc=1)
+    source = ref if source is None else source
+    side = net.copy(source.at[pl.ds(pl.multiple_of((1 - c) * 512, 512), 512), :], other, dc=1)
 
     def row(d, lo=0):
         return c * 512 + (t + d + 4) % 4 * 128 + lo
@@ -367,93 +368,9 @@
         scratch_shapes=list(scratch)
         + [pltpu.SemaphoreType.DMA((copies,)), pltpu.SemaphoreType.DMA((copies,)), pltpu.SemaphoreType.DMA((40,))],
         compiler_params=pltpu.CompilerParams(
-            collective_id=cid, has_side_effects=True, vmem_limit_bytes=56 * 2**20
+            collective_id=cid, has_side_effects=True, vmem_limit_bytes=61 * 2**20
         ),
     )(*[array for array, _ in ins])
-
-
-def grads_out(parts, cid):
-    def kernel(*refs):
-        parts_refs, out_ref, total = refs[:8], refs[8], refs[9]
-        bufs, (send, recv, local) = refs[10:-3], refs[-3:]
-        net = Net(send, recv)
-        loads = []
-        for k, ref in enumerate(parts_refs):
-            for x in range(4):
-                loads.append(
-                    pltpu.make_async_copy(
-                        ref.at[:, pl.ds(x * 512, 512)],
-                        total.at[x, pl.ds(STARTS[k], SIZES[k]), :],
-                        local.at[4 * k + x],
-                    )
-                )
-        for load in loads:
-            load.start()
-        net.greet(XZ_HOPS)
-        for load in loads:
-            load.wait()
-
-        def out(at, value):
-            out_ref[at, :] = value
-
-        for stage in scatter_weights(net, total, 0, ROWS, bufs, out):
-            stage()
-
-    (out,) = call(
-        kernel,
-        [(jax.ShapeDtypeStruct((ROWS, 128), F32), True)],
-        [(part, False) for part in parts],
-        [pltpu.VMEM((4, ROWS, 512), BF)] + scatter_shapes(ROWS),
-        16,
-        cid,
-    )
-    return out
-
-
-def rows_in(own, cid):
-    def kernel(own_ref, out_ref, rows, send, recv, local):
-        net = Net(send, recv)
-        at = pl.ds(pl.multiple_of(net.c * 512 + net.t * 128, 128), 128)
-        load = pltpu.make_async_copy(own_ref, rows.at[at, :], local.at[0])
-        load.start()
-        net.greet(Y_HOPS)
-        load.wait()
-        for stage in gather_rows(net, rows):
-            stage()
-        store = pltpu.make_async_copy(rows, out_ref, local.at[0])
-        store.start()
-        store.wait()
-
-    (out,) = call(
-        kernel, [(jax.ShapeDtypeStruct((SEQ, D), BF), False)], [(own, False)], [pltpu.VMEM((SEQ, D), BF)], 9, cid
-    )
-    return out
-
-
-def rows_out(part, cid):
-    def kernel(part_ref, out_ref, total, *rest):
-        bufs, (send, recv, local) = rest[:5], rest[5:]
-        net = Net(send, recv)
-        load = pltpu.make_async_copy(part_ref, total, local.at[0])
-        load.start()
-        net.greet(Y_HOPS)
-        load.wait()
-
-        def out(at, value):
-            out_ref[at, :] = value
-
-        for stage in scatter_rows(net, total, bufs, out):
-            stage()
-
-    (out,) = call(
-        kernel,
-        [(jax.ShapeDtypeStruct((128, D), F32), True)],
-        [(part, False)],
-        [pltpu.VMEM((SEQ, D), BF)] + ROW_BUFS,
-        5,
-        cid,
-    )
-    return out
 
 
 def dot(a, b, dims):
@@ -487,11 +404,11 @@
     return total
 
 
-def forward(piece, inputs, carried_state, attn_gain, mlp_gain, cosine, sine, row_mask, lam, cid):
+def forward(piece, inputs, carried_state, attn_gain, mlp_gain, cosine, sine, row_mask, lam, output_grad, cid):
     def kernel(
-        piece_ref, in_ref, carried_ref, gain_one, gain_two, cos_ref, sin_ref, mask_ref, lam_ref,
+        piece_ref, in_ref, carried_ref, gain_one, gain_two, cos_ref, sin_ref, mask_ref, lam_ref, grad_ref,
         weights_out, one_out, two_out, q_ref, k_ref, v_ref, s_ref, mix_ref, norm_ref, dev_ref, mixed_ref, prior_ref,
-        hidden_ref,
+        hidden_ref, grad_out,
         weights, one, two, carried, part, *rest,
     ):
         bufs, (send, recv, local) = rest[:5], rest[5:]
@@ -513,6 +430,7 @@
 
         norm_rows(in_ref, gain_one, one)
         net.greet(XZ_HOPS + Y_HOPS)
+        swap = net.copy(grad_ref, grad_out, dc=1)
         y1 = gather_rows(net, one)
         g1, g2, g3, g4 = (
             gather_weights(net, weights, lo, hi) for lo, hi in ((0, 1376), (1376, 1808), (1808, 2672), (2672, 3104))
@@ -523,6 +441,7 @@
         g1[1]()
         g1[2]()
         y1[1]()
+        swap.start()
         g2[0]()
         y1[2]()
         g2[1]()
@@ -538,7 +457,7 @@
                 ref[at, :128] = (former * cs - latter * sn).astype(BF)
                 ref[at, 128:] = (former * sn + latter * cs).astype(BF)
             v_ref[at, :] = (times(one, at, weights, 2) * mask_ref[at, :]).astype(BF)
-            s_ref[at, :] = times(one, at, weights, 3)
+            s_ref[at, :] = times(one, at, weights, 3).astype(BF)
 
         loop(SEQ, 256, project)
         g2[3]()
@@ -567,9 +486,9 @@
                 retained = dot(mixing, v_ref[keys, :], NN) + dot(q_ref[at, :], prior_ref[stretch], NN) * head
                 centred, dev = normal(retained, VDIM)
                 normed = centred * dev
-                norm_ref[at, :] = normed
+                norm_ref[at, :] = normed.astype(BF)
                 dev_ref[at, :] = dev
-                swish = s_ref[at, :]
+                swish = s_ref[at, :].astype(F32)
                 mixed_ref[at, :] = (mask_ref[at, :] * (swish * jax.nn.sigmoid(swish)) * normed).astype(BF)
 
             loop(HALF, 128, retain)
@@ -613,6 +532,7 @@
         store_two = pltpu.make_async_copy(two, two_out, local.at[3])
         store_two.start()
         g4[4]()
+        swap.wait()
         stores = [store_one, store_two]
         for x in range(4):
             store = pltpu.make_async_copy(weights.at[x], weights_out.at[:, pl.ds(x * 512, 512)], local.at[4 + x])
@@ -633,13 +553,14 @@
             (shape(SEQ, KDIM), True),
             (shape(SEQ, KDIM), True),
             (shape(SEQ, VDIM), True),
-            (shape(SEQ, VDIM, kind=F32), True),
+            (shape(SEQ, VDIM), True),
             (shape(SEQ, HALF), True),
-            (shape(SEQ, VDIM, kind=F32), True),
+            (shape(SEQ, VDIM), True),
             (shape(SEQ, 1, kind=F32), True),
             (shape(SEQ, VDIM), True),
             (shape(2, KDIM, VDIM), True),
             (shape(128, D, kind=F32), True),
+            (shape(HALF, D), False),
         ],
         [
             (piece, False),
@@ -651,6 +572,7 @@
             (sine, True),
             (row_mask, True),
             (lam, True),
+            (output_grad, False),
         ],
         [
             pltpu.VMEM((4, ROWS, 512), BF),
@@ -665,16 +587,472 @@
     )
 
 
-def layer_norm(rows_in, gain):
-    centre = jnp.mean(rows_in, axis=-1, keepdims=True)
-    centred = rows_in - centre
-    spread = jnp.mean(centred * centred, axis=-1, keepdims=True)
-    return centred * lax.rsqrt(spread + EPSILON) * gain
-
-
-def rotate(field, cosine, sine):
-    former, latter = field[:, :128], field[:, 128:]
-    return jnp.concatenate([former * cosine - latter * sine, former * sine + latter * cosine], axis=1)
+def transpose_to(ref, source):
+    for lo in range(0, SEQ, 256):
+        ref[:, lo : lo + 256] = source[lo : lo + 256, :].astype(F32).T.astype(BF)
+
+
+def weight_grad(flipped, rows_ref, out, start, count):
+    for x in range(4):
+
+        def body(cols, x=x):
+            at = pl.ds(pl.multiple_of(x * 512 + cols.start, 256), 256)
+            out[x, start : start + count, cols] = dot(flipped[...], rows_ref[:, at], NN).astype(BF)
+
+        loop(512, 256, body)
+
+
+def times_plain(pairs, x):
+    total = None
+    for rows, weights, start, count in pairs:
+        part = dot(rows, weights[x, start : start + count, :], NN)
+        total = part if total is None else total + part
+    return total
+
+
+def times_flipped(rows_ref, at, weights, start, count):
+    total = None
+    for x in range(4):
+        part = dot(rows_ref[at, x * 512 : x * 512 + 512], weights[x, start : start + count, :], NT)
+        total = part if total is None else total + part
+    return total
+
+
+def load_weights(source, weights, local, base, pieces):
+    loads = []
+    for k, (lo, to, rows) in enumerate(pieces):
+        for x in range(4):
+            loads.append(
+                pltpu.make_async_copy(
+                    source.at[pl.ds(lo, rows), pl.ds(x * 512, 512)],
+                    weights.at[x, pl.ds(to, rows), :],
+                    local.at[base + 4 * k + x],
+                )
+            )
+    for load in loads:
+        load.start()
+    return [loads[4 * k : 4 * k + 4] for k in range(len(pieces))]
+
+
+def wait_all(copies):
+    for copy in copies:
+        copy.wait()
+
+
+def norm_back(source, gain, grad, out):
+    def body(i, total):
+        at = pl.ds(pl.multiple_of(i * 32, 32), 32)
+        centred, dev = normal(source(at), D)
+        normed = centred * dev
+        back = grad(at)
+        scaled = back * gain[...]
+        mean = jnp.sum(scaled, axis=-1, keepdims=True) * (1.0 / D)
+        along = jnp.sum(scaled * normed, axis=-1, keepdims=True) * (1.0 / D)
+        out(at, dev * (scaled - mean - normed * along))
+        return total + jnp.sum(back * normed, axis=0, keepdims=True)
+
+    return lax.fori_loop(0, 4, body, jnp.zeros((1, D), F32))
+
+
+def mlp_back(weights_all, rows_two, grad_own, grad_other, hidden, mlp_gain, cid):
+    def kernel(
+        w_ref, two_ref, own_ref, other_ref, hidden_ref, gain,
+        mid_out, down_out, grad_hidden, gain_out, sums_out,
+        weights, two, grads, mid, part, act, gate_grad, up_grad, flipped, total,
+        *rest,
+    ):
+        row_bufs, (send, recv, local) = rest[:5], rest[-3:]
+        bufs = rest[5:-3]
+        net = Net(send, recv)
+        c, t = net.c, net.t
+        load_two = pltpu.make_async_copy(two_ref, two, local.at[0])
+        load_two.start()
+        load_g, load_u, load_d = load_weights(
+            w_ref, weights, local, 4, ((STARTS[5], 0, 432), (STARTS[6], 432, 432), (STARTS[7], 864, 432))
+        )
+        mine, theirs = (pl.ds(pl.multiple_of(k * HALF, HALF), HALF) for k in (c, 1 - c))
+        load_own = pltpu.make_async_copy(own_ref, grads.at[mine, :], local.at[1])
+        load_other = pltpu.make_async_copy(other_ref, grads.at[theirs, :], local.at[2])
+        load_own.start()
+        load_other.start()
+        net.greet(XZ_HOPS + Y_HOPS)
+        wait_all([load_two, *load_g, *load_u, *load_d, load_own, load_other])
+
+        def mlp_rows(base):
+            def body(rows):
+                at = pl.ds(pl.multiple_of(base + rows.start, rows.size), rows.size)
+                gate = times_flipped(two, at, weights, 0, 432)
+                up = times_flipped(two, at, weights, 432, 432)
+                back = times_flipped(grads, at, weights, 864, 432)
+                share = 0.5 + 0.5 * lax.erf(gate * 0.7071067811865476)
+                slope = share + gate * (0.3989422804014327 * jnp.exp(-0.5 * gate * gate))
+                gelu = gate * share
+                act[at, :] = (gelu * up).astype(BF)
+                gate_grad[at, :] = (back * up * slope).astype(BF)
+                up_grad[at, :] = (back * gelu).astype(BF)
+                for x in range(4):
+                    pairs = ((gate_grad[at, :], weights, 0, 432), (up_grad[at, :], weights, 432, 432))
+                    part[at, x * 512 : x * 512 + 512] = times_plain(pairs, x).astype(BF)
+
+            loop(HALF, 256, body)
+
+        def take(at, value):
+            total[at, :] = value
+
+        r1 = scatter_rows(net, part, row_bufs, take)
+        mid_stages = gather_rows(net, mid)
+        split = len(scatter_shapes(864))
+        sums = [
+            scatter_weights(
+                net, weights, lo, hi, some, lambda at, value: sums_out.__setitem__((at, slice(None)), value)
+            )
+            for lo, hi, some in ((0, 864, bufs[:split]), (864, 1296, bufs[split:]))
+        ]
+        mlp_rows((1 - c) * HALF)
+        r1[0]()
+        mlp_rows(c * HALF)
+        r1[1]()
+        transpose_to(flipped, gate_grad)
+        weight_grad(flipped, two, weights, 0, 432)
+        transpose_to(flipped, up_grad)
+        weight_grad(flipped, two, weights, 432, 432)
+        sums[0][0]()
+        r1[2]()
+        sums[0][1]()
+        r1[3]()
+
+        own = c * 512 + t * 128
+        def store(at, value):
+            to = pl.ds(pl.multiple_of(own + at.start, 32), 32)
+            whole = grads[to, :].astype(F32) + value
+            grad_hidden[at, :] = whole
+            mid[to, :] = whole.astype(BF)
+
+        gain_out[...] = norm_back(lambda at: hidden_ref[at, :], gain, lambda at: total[at, :], store)
+        mid_stages[0]()
+
+        def down_rows(at):
+            for x in range(4):
+                part[at, x * 512 : x * 512 + 512] = times_plain(((act[at, :], weights, 864, 432),), x).astype(BF)
+
+        loop(SEQ, 256, down_rows)
+        save_down = pltpu.make_async_copy(part, down_out, local.at[3])
+        save_down.start()
+        transpose_to(flipped, act)
+        weight_grad(flipped, grads, weights, 864, 432)
+        sums[1][0]()
+        sums[0][2]()
+        mid_stages[1]()
+        sums[1][1]()
+        sums[0][3]()
+        sums[1][2]()
+        sums[0][4]()
+        mid_stages[2]()
+        save_mid = pltpu.make_async_copy(mid, mid_out, local.at[1])
+        save_mid.start()
+        sums[1][3]()
+        sums[1][4]()
+        save_down.wait()
+        save_mid.wait()
+
+    def shape(*dims, kind=BF):
+        return jax.ShapeDtypeStruct(dims, kind)
+
+    return call(
+        kernel,
+        [
+            (shape(SEQ, D), False),
+            (shape(SEQ, D), False),
+            (shape(128, D, kind=F32), True),
+            (shape(1, D, kind=F32), True),
+            (shape(1296, 128, kind=F32), True),
+        ],
+        [
+            (weights_all, False),
+            (rows_two, False),
+            (grad_own, False),
+            (grad_other, False),
+            (hidden, True),
+            (mlp_gain, True),
+        ],
+        [
+            pltpu.VMEM((4, 1296, 512), BF),
+            pltpu.VMEM((SEQ, D), BF),
+            pltpu.VMEM((SEQ, D), BF),
+            pltpu.VMEM((SEQ, D), BF),
+            pltpu.VMEM((SEQ, D), BF),
+            pltpu.VMEM((SEQ, VDIM), BF),
+            pltpu.VMEM((SEQ, VDIM), BF),
+            pltpu.VMEM((SEQ, VDIM), BF),
+            pltpu.VMEM((VDIM, SEQ), BF),
+            pltpu.VMEM((128, D), F32),
+        ]
+        + ROW_BUFS
+        + scatter_shapes(864)
+        + scatter_shapes(432),
+        64,
+        cid,
+    )
+
+
+GRAD_HOPS = (dict(dx=2), dict(dz=2), dict(dt=2))
+
+
+def retention_back(
+    weights_all, rows_mid, rows_one, down_part, mixed, q, k, v, s, normed, dev, mix, prior, hidden, grad_hidden, inputs,
+    attn_gain, cosine, sine, row_mask, lam, mlp_gain_part, sums_mlp, cid
+):
+    places = ((STARTS[4], 0, 432), (STARTS[3], 432, 432), (STARTS[2], 864, 432), (0, 1296, 256), (256, 1552, 256))
+
+    def kernel(
+        w_ref, mid_ref, one_ref, down_ref, mixed_ref, q_ref, k_ref, v_ref, s_ref, norm_ref, dev_ref, mix_ref,
+        prior_ref, hidden_ref, gh_ref, in_ref, gain, cos_ref, sin_ref, mask_ref, lam_ref, mlp_gain_ref, sums_mlp_ref,
+        out_ref, in_grad, gains_out, sums_out, sums_got, mlp_got,
+        weights, one, mid, down, swish_grad, ret_grad, q_grad, k_grad, v_grad, score_grad, flipped, total,
+        by_core, by_t, by_x, by_z,
+        *rest,
+    ):
+        first_bufs, second_bufs, (send, recv, local) = rest[:5], rest[5:10], rest[-3:]
+        bufs = rest[10:-3]
+        net = Net(send, recv)
+        c, t = net.c, net.t
+        load_mid = pltpu.make_async_copy(mid_ref, mid, local.at[0])
+        load_mid.start()
+        load_o, load_s, load_v, load_q, load_k = load_weights(w_ref, weights, local, 8, places)
+        mine = pl.ds(pl.multiple_of(c * HALF, HALF), HALF)
+        load_down = pltpu.make_async_copy(down_ref.at[mine, :], down.at[mine, :], local.at[1])
+        load_down.start()
+        load_one = pltpu.make_async_copy(one_ref, one, local.at[2])
+        load_one.start()
+        net.greet(XZ_HOPS + Y_HOPS + GRAD_HOPS)
+        send_mlp = net.copy(sums_mlp_ref, mlp_got, dc=1)
+        send_mlp.start()
+
+        def take_out(at, value):
+            out_ref[at, :] = (hidden_ref[at, :] + value).astype(BF)
+
+        def take(at, value):
+            total[at, :] = value
+
+        r1 = scatter_rows(net, down, first_bufs, take_out, source=down_ref)
+        r1[0]()
+        load_down.wait()
+        wait_all([load_mid, *load_o])
+
+        def gate_back(at):
+            back = times_flipped(mid, at, weights, 0, 432) * mask_ref[at, :]
+            swish = s_ref[at, :].astype(F32)
+            normed = norm_ref[at, :].astype(F32)
+            share = jax.nn.sigmoid(swish)
+            swish_grad[at, :] = (back * normed * (share * (1.0 + swish * (1.0 - share)))).astype(BF)
+            back = back * (swish * share)
+            mean = jnp.sum(back, axis=-1, keepdims=True) * (1.0 / VDIM)
+            along = jnp.sum(back * normed, axis=-1, keepdims=True) * (1.0 / VDIM)
+            ret_grad[at, :] = ((back - mean - normed * along) * dev_ref[at, :]).astype(BF)
+
+        loop(SEQ, 256, gate_back)
+        r1[1]()
+        split = [0]
+        for rows in (432, 864, 512):
+            split.append(split[-1] + len(scatter_shapes(rows)))
+
+        def put(at, value):
+            sums_out[at, :] = value
+
+        wait_all(load_s)
+        sums = [
+            scatter_weights(net, weights, lo, hi, bufs[split[i] : split[i + 1]], put)
+            for i, (lo, hi) in enumerate(((0, 432), (432, 1296), (1296, 1808)))
+        ]
+        transpose_to(flipped, mixed_ref)
+        weight_grad(flipped, mid, weights, 0, 432)
+        sums[0][0]()
+
+        decay = lam_ref[0:1, 0:1]
+        far = lax.broadcasted_iota(jnp.int32, (HALF, 1), 0).astype(F32)
+        tail = jnp.exp((HALF - 1.0 - far) * decay)
+        head_all = jnp.exp((far + 1.0) * decay)
+        ahead = (q_ref[HALF:, :].astype(F32) * head_all).astype(BF)
+        grad_local = dot(ahead, ret_grad[HALF:, :], TN).astype(BF)
+
+        def turn_back(at, raw):
+            cs, sn = cos_ref[at, :], sin_ref[at, :]
+            former, latter = raw[:, :128], raw[:, 128:]
+            return (former * cs + latter * sn).astype(BF), (latter * cs - former * sn).astype(BF)
+
+        for stretch in range(2):
+            keys = slice(stretch * HALF, stretch * HALF + HALF)
+
+            def score_rows(rows, stretch=stretch, keys=keys):
+                at = pl.ds(pl.multiple_of(stretch * HALF + rows.start, rows.size), rows.size)
+                n = lax.broadcasted_iota(jnp.int32, (rows.size, HALF), 0) + rows.start
+                distance = (n - lax.broadcasted_iota(jnp.int32, (rows.size, HALF), 1)).astype(F32)
+                fade = jnp.where(distance >= 0.0, jnp.exp(jnp.maximum(distance, 0.0) * decay), 0.0)
+                scores = (dot(ret_grad[at, :], v_ref[keys, :], NT) * fade).astype(BF)
+                score_grad[rows, :] = scores
+                step = lax.broadcasted_iota(jnp.int32, (rows.size, 1), 0) + rows.start + 1
+                head = jnp.exp(step.astype(F32) * decay)
+                raw = dot(scores, k_ref[keys, :], NN) + dot(ret_grad[at, :], prior_ref[stretch], NT) * head
+                q_grad[at, :128], q_grad[at, 128:] = turn_back(at, raw)
+
+            loop(HALF, 128, score_rows)
+            raw = dot(score_grad[...], q_ref[keys, :], TN)
+            value = dot(mix_ref[keys, :], ret_grad[keys, :], TN)
+            if stretch == 0:
+                raw = raw + dot(v_ref[keys, :], grad_local, NT) * tail
+                value = value + dot(k_ref[keys, :], grad_local, NN) * tail
+            k_grad[keys, :128], k_grad[keys, 128:] = turn_back(keys, raw)
+            v_grad[keys, :] = (value * mask_ref[keys, :]).astype(BF)
+
+        r1[2]()
+        sums[0][1]()
+        wait_all(load_v + load_q + load_k)
+        part = mid
+
+        def back_rows(base):
+            def body(rows):
+                at = pl.ds(pl.multiple_of(base + rows.start, rows.size), rows.size)
+                pairs = (
+                    (swish_grad[at, :], weights, 432, 432),
+                    (v_grad[at, :], weights, 864, 432),
+                    (q_grad[at, :], weights, 1296, 256),
+                    (k_grad[at, :], weights, 1552, 256),
+                )
+                for x in range(4):
+                    part[at, x * 512 : x * 512 + 512] = times_plain(pairs, x).astype(BF)
+
+            loop(HALF, 256, body)
+
+        r2 = scatter_rows(net, part, second_bufs, take)
+        back_rows((1 - c) * HALF)
+        r2[0]()
+        back_rows(c * HALF)
+        r1[3]()
+        load_one.wait()
+        transpose_to(flipped, swish_grad)
+        weight_grad(flipped, one, weights, 432, 432)
+        r2[1]()
+        sums[0][2]()
+        transpose_to(flipped, v_grad)
+        weight_grad(flipped, one, weights, 864, 432)
+        sums[1][0]()
+        sums[0][3]()
+        transpose_to(flipped.at[0:256], q_grad)
+        weight_grad(flipped.at[0:256], one, weights, 1296, 256)
+        transpose_to(flipped.at[0:256], k_grad)
+        weight_grad(flipped.at[0:256], one, weights, 1552, 256)
+        sums[2][0]()
+        r2[2]()
+        sums[1][1]()
+        sums[0][4]()
+        sums[2][1]()
+        r2[3]()
+
+        def store(at, value):
+            in_grad[at, :] = gh_ref[at, :] + value
+
+        first = norm_back(lambda at: in_ref[at, :].astype(F32), gain, lambda at: total[at, :], store)
+
+        by_core[c, 0:1, :] = first
+        by_core[c, 1:2, :] = mlp_gain_ref[...]
+
+        def spread(ref, place, hops, axis):
+            copies = [net.copy(ref.at[place], ref.at[place], **{axis: hop}) for hop in hops]
+            for copy in copies:
+                copy.start()
+            return copies
+
+        def gathered(ref, copies, count):
+            for copy in copies:
+                copy.wait()
+            value = ref[0]
+            for k in range(1, count):
+                value = value + ref[k]
+            return value
+
+        near = spread(by_core, c, (1,), "dc")
+        by_t[t] = gathered(by_core, near, 2)
+        near = spread(by_t, t, (1, -1, 2), "dt")
+        sums[1][2]()
+        by_x[net.x] = gathered(by_t, near, 4)
+        near = spread(by_x, net.x, (1, -1, 2), "dx")
+        sums[2][2]()
+        by_z[net.z] = gathered(by_x, near, 4)
+        near = spread(by_z, net.z, (1, -1, 2), "dz")
+        sums[1][3]()
+        gains_out[...] = gathered(by_z, near, 4)
+        sums[2][3]()
+        sums[1][4]()
+        sums[2][4]()
+        send_sums = net.copy(sums_out, sums_got, dc=1)
+        send_sums.start()
+        send_mlp.wait()
+        send_sums.wait()
+
+    def shape(*dims, kind=BF):
+        return jax.ShapeDtypeStruct(dims, kind)
+
+    return call(
+        kernel,
+        [
+            (shape(128, D), True),
+            (shape(128, D, kind=F32), True),
+            (shape(2, D, kind=F32), True),
+            (shape(1808, 128, kind=F32), True),
+            (shape(1808, 128, kind=F32), True),
+            (shape(1296, 128, kind=F32), False),
+        ],
+        [
+            (weights_all, False),
+            (rows_mid, False),
+            (rows_one, False),
+            (down_part, False),
+            (mixed, True),
+            (q, True),
+            (k, True),
+            (v, True),
+            (s, True),
+            (normed, True),
+            (dev, True),
+            (mix, True),
+            (prior, True),
+            (hidden, True),
+            (grad_hidden, True),
+            (inputs, True),
+            (attn_gain, True),
+            (cosine, True),
+            (sine, True),
+            (row_mask, True),
+            (lam, True),
+            (mlp_gain_part, True),
+            (sums_mlp, False),
+        ],
+        [
+            pltpu.VMEM((4, 1808, 512), BF),
+            pltpu.VMEM((SEQ, D), BF),
+            pltpu.VMEM((SEQ, D), BF),
+            pltpu.VMEM((SEQ, D), BF),
+            pltpu.VMEM((SEQ, VDIM), BF),
+            pltpu.VMEM((SEQ, VDIM), BF),
+            pltpu.VMEM((SEQ, KDIM), BF),
+            pltpu.VMEM((SEQ, KDIM), BF),
+            pltpu.VMEM((SEQ, VDIM), BF),
+            pltpu.VMEM((HALF, HALF), BF),
+            pltpu.VMEM((VDIM, SEQ), BF),
+            pltpu.VMEM((128, D), F32),
+            pltpu.VMEM((2, 2, D), F32),
+            pltpu.VMEM((4, 2, D), F32),
+            pltpu.VMEM((4, 2, D), F32),
+            pltpu.VMEM((4, 2, D), F32),
+        ]
+        + ROW_BUFS
+        + ROW_BUFS
+        + scatter_shapes(432)
+        + scatter_shapes(864)
+        + scatter_shapes(512),
+        80,
+        cid,
+    )
 
 
 def swap_cores(array):
@@ -720,94 +1098,36 @@
     angles = position.astype(F32)[:, None] * frequency[None, :]
     cosine, sine = jnp.cos(angles), jnp.sin(angles)
     decay = -jnp.power(2.0, 5.0 - head.astype(F32)) / SEQ
-    (
-        weights, rows_one, rows_two, queries, keys_rot, values_kept, swish_raw, mix, normed, dev, mixed, prior, hidden
-    ) = forward(
-        piece, inputs, carried_state, attn_gain[None, :], mlp_gain[None, :], cosine, sine, row_mask,
-        jnp.full((8, 128), decay, F32), 1
+    gains = attn_gain[None, :], mlp_gain[None, :]
+    lam = jnp.full((8, 128), decay, F32)
+    weights, rows_one, rows_two, q, k, v, s, mix, normed, dev, mixed, prior, hidden, grad_other = forward(
+        piece, inputs, carried_state, *gains, cosine, sine, row_mask, lam, output_grad, 1
     )
-    w_query, w_key, w_value, w_swish, w_out, w_gate, w_up, w_down = (
-        weights[s : s + n] for s, n in zip(STARTS, SIZES)
+    rows_mid, down_part, grad_hidden, mlp_gain_part, sums_mlp = mlp_back(
+        weights, rows_two, output_grad, grad_other, hidden, gains[1], 2
     )
-    local_pos = jnp.arange(HALF).astype(F32)
-    tail_fac = jnp.exp((HALF - 1.0 - local_pos) * decay)[:, None]
-    head_fac = jnp.exp((local_pos + 1.0) * decay)[:, None]
-    distance = local_pos[:, None] - local_pos[None, :]
-    decay_mask = jnp.where(distance >= 0.0, jnp.exp(jnp.maximum(distance, 0.0) * decay), 0.0)
-    inputs_wide = inputs.astype(F32)
-    stretch = lambda a: (a[:HALF], a[HALF:])
-    qs, ks, vs, mixing = stretch(queries), stretch(keys_rot), stretch(values_kept), stretch(mix)
-    gate_pre = dot(rows_two, w_gate, NT)
-    up_pre = dot(rows_two, w_up, NT)
-
-    def mlp_piece(gate_in, up_in):
-        return jax.nn.gelu(gate_in, approximate=False) * up_in
-
-    activated = mlp_piece(gate_pre, up_pre).astype(BF)
-    outputs = (hidden + rows_out(dot(activated, w_down, NN).astype(BF), 5)).astype(BF)
-    grad_all = lax.all_gather(output_grad, "ctx", axis=0, tiled=True)
-    grad_own = lax.dynamic_slice_in_dim(output_grad, lax.axis_index("tp") * 128, 128, 0).astype(F32)
-    down_part = dot(activated, grad_all, TN)
-    grad_act = dot(grad_all, w_down, NT)
-    _, mlp_pull = jax.vjp(mlp_piece, gate_pre, up_pre)
-    grad_gate, grad_up = (g.astype(BF) for g in mlp_pull(grad_act))
-    gate_part = dot(grad_gate, rows_two, TN)
-    up_part = dot(grad_up, rows_two, TN)
-    grad_norm_two = rows_out((dot(grad_gate, w_gate, NN) + dot(grad_up, w_up, NN)).astype(BF), 6)
-    _, norm_two_pull = jax.vjp(layer_norm, hidden, mlp_gain)
-    grad_hidden_norm, mlp_gain_part = norm_two_pull(grad_norm_two)
-    grad_hidden = grad_own + grad_hidden_norm
-    mid_rows = rows_in(grad_hidden.astype(BF), 7)
-    out_part = dot(mixed, mid_rows, TN)
-    grad_mixed = dot(mid_rows, w_out, NT)
-    sig = jax.nn.sigmoid(swish_raw)
-    grad_swish = (row_mask * grad_mixed * normed * (sig * (1.0 + swish_raw * (1.0 - sig)))).astype(BF)
-    grad_normed = row_mask * grad_mixed * (swish_raw * sig)
-    grad_normed = grad_normed - jnp.mean(grad_normed, axis=-1, keepdims=True) - normed * jnp.mean(
-        grad_normed * normed, axis=-1, keepdims=True
+    outputs, input_grad, gain_grads, sums, got_sums, got_mlp = retention_back(
+        weights, rows_mid, rows_one, down_part, mixed, q, k, v, s, normed, dev, mix, prior, hidden, grad_hidden, inputs,
+        gains[0], cosine, sine, row_mask, lam, mlp_gain_part, sums_mlp, 3
     )
-    grad_retained = (grad_normed * dev).astype(BF)
-    rs = stretch(grad_retained)
-    grad_local = dot((qs[1] * head_fac).astype(BF), rs[1], TN).astype(BF)
-    gq, gk, gv = [], [], []
-    for at in (0, 1):
-        grad_scores = (dot(rs[at], vs[at], NT) * decay_mask).astype(BF)
-        gq.append(dot(grad_scores, ks[at], NN) + dot(rs[at], prior[at], NT) * head_fac)
-        gk.append(dot(grad_scores, qs[at], TN))
-        gv.append(dot(mixing[at], rs[at], TN))
-    gk[0] = gk[0] + dot(vs[0], grad_local, NT) * tail_fac
-    gv[0] = gv[0] + dot(ks[0], grad_local, NN) * tail_fac
-    grad_query = rotate(jnp.concatenate(gq, axis=0), cosine, -sine).astype(BF)
-    grad_key = rotate(jnp.concatenate(gk, axis=0), cosine, -sine).astype(BF)
-    grad_value = (jnp.concatenate(gv, axis=0) * row_mask).astype(BF)
-    four = (grad_query, grad_key, grad_value, grad_swish)
-    sums = [dot(g, rows_one, TN) for g in four]
-    total_rows = sum(dot(g, w, NN) for g, w in zip(four, (w_query, w_key, w_value, w_swish)))
-    grad_norm_one = rows_out(total_rows.astype(BF), 8)
-    _, norm_one_pull = jax.vjp(layer_norm, inputs_wide, attn_gain)
-    grad_inputs_norm, attn_gain_part = norm_one_pull(grad_norm_one)
-    input_grad = grad_hidden + grad_inputs_norm
-    attn_gain_grad, mlp_gain_grad = lax.psum((attn_gain_part, mlp_gain_part), ("fsdp", "ctx", "tp"))
-
-    summed = grads_out([part.astype(BF) for part in (*sums, out_part, gate_part, up_part, down_part)], 9)
-    left, right = summed[:, :64], summed[:, 64:]
-    mine = jnp.where(core == 0, left, right)
-    got = swap_cores(jnp.where(core == 0, right, left))
-    first, second = jnp.where(core == 0, mine, got), jnp.where(core == 0, got, mine)
+    own = jnp.where(core == 0, sums[:, :64], sums[:, 64:]), jnp.where(core == 0, sums_mlp[:, :64], sums_mlp[:, 64:])
+    got = jnp.where(core == 0, got_sums[:, :64], got_sums[:, 64:]), jnp.where(core == 0, got_mlp[:, :64], got_mlp[:, 64:])
+    places = ((0, 1296, 256), (0, 1552, 256), (0, 864, 432), (0, 432, 432), (0, 0, 432), (1, 0, 432), (1, 432, 432), (1, 864, 432))
     grads = []
-    for k, (s, n) in enumerate(zip(STARTS, SIZES)):
-        both = jnp.concatenate([first[s : s + n], second[s : s + n]], axis=0)
-        grads.append(both if k in (4, 7) else both.T)
+    for at, (which, lo, n) in enumerate(places):
+        a, b = own[which][lo : lo + n], got[which][lo : lo + n]
+        both = jnp.where(core == 0, jnp.concatenate([a, b], axis=0), jnp.concatenate([b, a], axis=0))
+        grads.append(both if at in (4, 7) else both.T)
     return (
         outputs,
         input_grad,
-        attn_gain_grad,
+        gain_grads[0],
         grads[0],
         grads[1],
         grads[2],
         grads[3],
         grads[4],
-        mlp_gain_grad,
+        gain_grads[1],
         grads[5],
         grads[6],
         grads[7],

time: 579 us -> 318 us (0.55); the launches traced: 570 us -> 317 us
  matrix products: 109 us -> 0 us
  blocking collectives: 65.8 us -> 0 us
  Pallas kernels: 330 us -> 286 us
  other arithmetic: 28.2 us -> 9.97 us
  between operations: 16 us -> 1.65 us
    dot_general x32 -> x0, matrix products: 109 us -> none  [dot(): return lax.dot_general(a, b, (dims, ((), ())), preferred_element_type=F32)]
    psum x1 -> x0, blocking collectives: 65.8 us -> none  [on_device(): lax.psum((attn_gain_part, mlp_gain_part), ('fsdp', 'ctx', 'tp'))]
    pallas_call x6 -> x3, Pallas kernels: 330 us -> 286 us  [call(): pl.pallas_call(kernel, out_shape=[shape for shape, _ in outs], in_specs=[...]
    reduce_sum x8 -> x0, other arithmetic: 8.84 us -> none  [the longest x2 2.26 us: layer_norm(): return centred * lax.rsqrt(spread + EPSILON) * gain]
    unnamed x86 -> x38, local copies, waits for them, and re-layouts: 10.9 us -> 11.6 us
  transfers between devices with their start and end apart: 3 -> 1, of which waited for: 0 -> 0; matrix products, arithmetic and copies ran while one was open for 6% -> 2% of each run, Pallas kernels for 26% -> 0%
where the time goes in v3:
time: 318 us; the launch traced here: 317 us
  Pallas kernels  286 us (90%)
  local copies, waits for them, and re-layouts  18 us (6%)
  other arithmetic  9.97 us (3%)
    pallas_call x3, Pallas kernels, call(): pl.pallas_call(kernel, out_shape=[shape for shape, _ in outs], in_specs=[...  286 us
    unnamed x38, local copies, waits for them, and re-layouts  11.6 us
  transfers between devices with their start and end apart: 1, of which 0 were waited for; matrix products, arithmetic and copies ran while one was open for 2% of the time, Pallas kernels for 0%

profile of v3, /device:TPU:1, one launch (start us, length us, event | category | flops | bytes accessed | tf_op | source)
XLA Modules:
  0.0 317.2 jit_solution(8235301577271818348)
XLA Ops:
  0.7 1.1 constant_dynamic-slice_fusion.6
  1.8 1.1 constant_dynamic-slice_fusion.2
  2.9 1.1 constant_dynamic-slice_fusion.3
  4.1 0.9 constant_dynamic-slice_fusion.8
  5.2 1.6 collective-permute-start
  8.8 1.3 copy.61.carried_ref
  10.1 0.8 fusion.mask_ref
  10.9 3.0 multiply_sine_fusion
  14.4 1.8 maximum_select_fusion.piece_ref
  16.7 122.0 %shard_map.229 = (bf16[3104,2048]{1,0:T(8,128)(2,1)}, bf16[1024,2048]{1,0:T(8,128)(2,1)}, bf16[1024,2048]{1,0:T(8,128)(2,1)}, bf16[1024,256]{1,0:T(8,128)(2,1)},...) custom-call(bf16[3104,128]{1,0:T(8,128)(2,1)} %maximum_select_fusion, ...), custom_call_target="tpu_custom_call" | custom-call | tf_op jit(solution)/shard_map/pallas_call | solution.py:363
  138.7 74.6 %shard_map.230 = (bf16[1024,2048]{1,0:T(8,128)(2,1)}, bf16[1024,2048]{1,0:T(8,128)(2,1)}, f32[128,2048]{1,0:T(8,128)}, f32[1,2048]{1,0:T(1,128)}, f32[1296,128]{1,0:T(8,128)}) custom-call(bf16[3104,2048]{1,0:T(8,128)(2,1)} %get-tuple-element.37.w_ref, bf16[1024,2048]{1,0:T(8,128)(2,1)} %get-tuple-element.38.two_ref, bf16[512,2048]{1,0:T(8,128)(2,1)} %own_ref.1, ...), custom_call_target="tpu_custom_call" | custom-call | tf_op jit(solution)/shard_map/pallas_call | solution.py:363
  213.3 1.5 slice_select_fusion.3
  214.8 89.5 %shard_map.231 = (bf16[128,2048]{1,0:T(8,128)(2,1)}, f32[128,2048]{1,0:T(8,128)}, f32[2,2048]{1,0:T(2,128)}, f32[1808,128]{1,0:T(8,128)}, f32[1808,128]{1,0:T(8,128)}, /*index=5*/f32[1296,128]{1,0:T(8,128)}) custom-call(bf16[3104,2048]{1,0:T(8,128)(2,1)} %get-tuple-element.37.w_ref, bf16[1024,2048]{1,0:T(8,128)(2,1)} %get-tuple-element.41.mid_ref, ...), custom_call_target="tpu_custom_call" | custom-call | tf_op jit(solution)/shard_map/pallas_call | solution.py:363
  304.3 1.8 slice_select_fusion.1
  308.3 0.9 copy.69
  309.2 0.9 copy.68
  310.1 0.9 copy.67
  311.1 0.9 copy.66
  312.0 0.8 copy.63
  312.8 0.8 copy.62
  313.6 0.9 copy.65
  314.5 0.9 copy.64
  315.4 0.8 copy.88
  316.2 1.0 copy.89
  (51 shorter events, 4.8 us)
Async XLA Ops:
  4.0 4.7 %copy-start.3 = (f32[1,2,256,432]{2,3,1,0:T(8,128)S(1)}, f32[1,2,256,432]{2,3,1,0:T(8,128)}, u32[]{:S(2)}) copy-start(f32[1,2,256,432]{2,3,1,0:T(8,128)} %param.16) | copy-start | bytes 2654212
  5.2 8.7 %collective-permute-start = (bf16[3104,64]{0,1:T(8,128)(2,1)S(1)}, bf16[3104,64]{0,1:T(8,128)(2,1)S(1)}, u32[]{:S(2)}, u32[]{:S(2)}) collective-permute-start(bf16[3104,64]{0,1:T(8,128)(2,1)S(1)} %concatenate.61), channel_id=1, source_target_pairs={{0,4},{4,0},{1,5},{5,1},{2,6},{6,2},{3,7},{7,3},{8,12},{12,8},{9,1... | collective-permute-start | bytes 1191944 | tf_op jit(solution)/shard_map/ppermute | solution.py:1059
  304.3 1.9 copy-start
  306.6 0.7 copy-start.5
  306.6 1.3 copy-start.1
  312.7 2.7 copy-start.4
  313.6 2.7 copy-start.2
